TPU v7x, 512 devices: a whole 4x8x8 slice. The times are simulated.
512 devices in a mesh: grp: 16 (over y, core), graph: 32 (over x, z).
Axes of the slice: x: 4, y: 8, z: 8, core: 2. Of those that a mesh axis runs over, the one named last changes fastest.
Arguments:
- atoms: bfloat16 [16, 128, 9, 512], P('grp', 'graph'), may hold values from -6 to 6
- cotangent: bfloat16 [16, 128, 9, 512], P('grp', 'graph'), may hold values from -0.75 to 0.75
- expert_weights: bfloat16 [32, 3, 512, 512], P('grp', None, 'graph'), may hold values from -1 to 1
- coefficients: int32 [16, 32], replicated, may hold values from 1 to 256, 1024 in all within a row
- src_owner: int32 [16, 4096, 1], P('grp', 'graph'), may hold values from 0 to 31; in each aligned block of 128 rows (0 to 127, 128 to 255, ..., all dimensions but the last counted through in order) at most 6 rows name the same one
- src_slot: int32 [16, 4096], P('grp', 'graph'), may hold values from 0 to 3
- tgt_slot: int32 [16, 4096], P('grp', 'graph'), may hold values from 0 to 3
- rot_index: int32 [16, 4096], P('grp', 'graph'), may hold values from 0 to 63
- rot_table: float32 [64, 9, 9], replicated, may hold values from -3 to 3, as said below
Outputs:
- grad_atoms: float32 [16, 128, 9, 512], P('grp', 'graph')
- grad_experts: float32 [32, 3, 512, 512], P('grp', None, 'graph')
Inputs may be any that keep to these rules, and one draw needn't show every extreme that they name: `src_owner`: among the 128 edges of one index of graph (aligned blocks of rows), no owner is named more than 6 times, a bound that some block reaches. `coefficients`: each row sums to 1024. Every rot_table[r] is block diagonal with blocks over coefficients 0, 1..3 and 4..8.
All inputs are finite; a program needn't handle non-finite values.
Results may differ from a plain program's by a relative error of at most 0.035.
Values may be sent and summed in bfloat16 or wider, within the bound.
A program may use at most 64 MiB of HBM per device.

v0:
```python
import jax
import jax.numpy as jnp
from jax import lax
from jax.sharding import PartitionSpec as P

precise = lax.Precision.HIGHEST
degree_spans = ((0, 1), (1, 4), (4, 9))


def per_degree(operand, matrices, flipped):
    pieces = []
    contracted = 1 if flipped else 0
    for degree in range(3):
        opening, closing = degree_spans[degree]
        segment = operand[:, opening:closing, :]
        flattened = segment.reshape(-1, segment.shape[-1])
        product = lax.dot_general(
            flattened,
            matrices[degree],
            (((1,), (contracted,)), ((), ())),
            preferred_element_type=jnp.float32,
        )
        pieces.append(product.reshape(segment.shape[0], closing - opening, -1))
    return jnp.concatenate(pieces, axis=1)


def rotate(rotations, values, flipped):
    form = "eba,ebc->eac" if flipped else "eab,ebc->eac"
    return jnp.einsum(form, rotations, values.astype(jnp.float32), precision=precise)


def shards(
    atoms,
    cotangent,
    expert_weights,
    coefficients,
    src_owner,
    src_slot,
    tgt_slot,
    rot_index,
    rot_table,
):
    peer_count = lax.axis_size("graph")
    own_count = expert_weights.shape[0]
    local_atoms = atoms.shape[1]
    channels = atoms.shape[-1]
    edge_count = src_slot.shape[1]
    shares = coefficients.astype(jnp.float32) / 1024.0
    own_shares = lax.dynamic_slice_in_dim(shares, lax.axis_index("grp") * own_count, own_count, 1)
    narrow_shares = own_shares.astype(jnp.bfloat16)
    mixed_rows = lax.psum_scatter(
        jnp.einsum(
            "sk,klab->slab", narrow_shares, expert_weights, preferred_element_type=jnp.float32
        ).astype(jnp.bfloat16),
        "grp",
        scatter_dimension=0,
        tiled=True,
    ).astype(jnp.float32)
    mixed = lax.all_gather(mixed_rows[0].astype(jnp.bfloat16), "graph", axis=1, tiled=True)
    gathered = lax.all_gather(atoms, "graph", axis=1, tiled=True)[0]
    owners = src_owner[0, :, 0]
    sources = owners * local_atoms + src_slot[0]
    table_count = rot_table.shape[0]
    rot_pick = (rot_index[0][:, None] == jnp.arange(table_count, dtype=jnp.int32)[None, :]).astype(
        jnp.float32
    )
    rotations = jnp.dot(rot_pick, rot_table.reshape(table_count, 81), precision=precise).reshape(
        edge_count, 9, 9
    )
    leading = (jnp.arange(9) == 0).astype(jnp.float32)[None, :, None]
    own_cotangent = cotangent[0]
    block_rows = min(256, edge_count)
    weight_terms = [jnp.zeros((channels, channels), jnp.float32) for degree in range(3)]
    rotated = rotate(rotations, gathered[sources], False).astype(jnp.bfloat16)
    hidden = per_degree(rotated, mixed, False)
    gates = jax.nn.sigmoid(hidden[:, 0:1, :])
    msg_grads = rotate(rotations, own_cotangent[tgt_slot[0, 0:block_rows]], False)
    gate_terms = jnp.sum(msg_grads * hidden, axis=1, keepdims=True) * gates * (1.0 - gates)
    hidden_grads = (msg_grads * gates + leading * gate_terms).astype(jnp.bfloat16)
    for degree in range(3):
        opening, closing = degree_spans[degree]
        lefts = rotated[:, opening:closing, :].reshape(-1, channels)
        rights = hidden_grads[:, opening:closing, :].reshape(-1, channels)
        weight_terms[degree] = lax.dot_general(
            lefts, rights, (((0,), (0,)), ((), ())), preferred_element_type=jnp.float32
        )
    rot_grads = per_degree(hidden_grads, mixed, True)
    edge_pieces = rotate(rotations, rot_grads, True).astype(jnp.bfloat16)
    weight_rows = lax.psum_scatter(
        jnp.stack(weight_terms).astype(jnp.bfloat16), "graph", scatter_dimension=1, tiled=True
    ).astype(jnp.float32)
    system_rows = lax.all_gather(
        weight_rows[None].astype(jnp.bfloat16), "grp", axis=0, tiled=True
    ).astype(jnp.float32)
    grad_experts = jnp.einsum("sk,slab->klab", own_shares, system_rows, precision=precise)
    capacity = 3 * edge_count // (2 * peer_count)
    member = (owners[:, None] == jnp.arange(peer_count, dtype=jnp.int32)[None, :]).astype(jnp.int32)
    positions = jnp.sum(jnp.cumsum(member, axis=0) * member, axis=1) - 1
    outgoing = (
        jnp.zeros((peer_count, capacity, 9, channels), jnp.bfloat16)
        .at[owners, positions]
        .set(edge_pieces)
    )
    slot_ids = (
        jnp.full((peer_count, capacity), local_atoms, jnp.int32)
        .at[owners, positions]
        .set(src_slot[0])
    )
    incoming, incoming_slots = (
        lax.all_to_all(outgoing, "graph", split_axis=0, concat_axis=0, tiled=True),
        lax.all_to_all(slot_ids, "graph", split_axis=0, concat_axis=0, tiled=True),
    )
    selector = (
        incoming_slots.reshape(-1)[:, None] == jnp.arange(local_atoms, dtype=jnp.int32)[None, :]
    ).astype(jnp.bfloat16)
    atom_grads = lax.dot_general(
        selector,
        incoming.reshape(-1, 9 * channels),
        (((0,), (0,)), ((), ())),
        preferred_element_type=jnp.float32,
    ).reshape(local_atoms, 9, channels)
    return (atom_grads[None], grad_experts)


def solution(mesh):
    placed = (
        P("grp", "graph", None, None),
        P("grp", "graph", None, None),
        P("grp", None, "graph", None),
        P(),
        P("grp", "graph", None),
        P("grp", "graph"),
        P("grp", "graph"),
        P("grp", "graph"),
        P(),
    )
    return jax.shard_map(
        shards,
        mesh=mesh,
        in_specs=placed,
        out_specs=(P("grp", "graph", None, None), P("grp", None, "graph", None)),
        check_vma=False,
    )
```

profile of v0, /device:TPU:1, one launch (start us, length us, event | category | flops | bytes accessed | tf_op | source)
XLA Modules:
  0.0 470.1 jit_solution(1796639803038937812)
XLA Ops:
  8.1 0.8 copy-done
  8.9 1.1 convolution_convert_fusion.1
  10.0 1.3 copy.107
  11.4 0.0 all-gather.5.cloned.1.call-start
  11.5 0.6 copy.103
  12.2 63.0 %reduce-scatter.3.cloned.1.call-done = bf16[1,3,16,512]{3,2,1,0:T(8,128)(2,1)} async-done(((bf16[16,3,16,512]{3,2,1,0:T(8,128)(2,1)}), bf16[1,3,16,512]{3,2,1,0:T(8,128)(2,1)}) %reduce-scatter.3.cloned.1.call-update) | async-done | bytes 49168 | tf_op jit(solution)/shard_map/reduce_scatter | solution.py:51
  75.2 0.1 fusion.27
  75.3 0.2 reduce_window_sum.11
  75.4 0.2 select_reduce_fusion
  75.6 6.4 %scatter_fusion = s32[32,6]{0,1:T(8,128)S(1)} fusion(s32[32,6]{0,1:T(8,128)S(1)} %broadcast_in_dim.4, s32[128]{0:T(128)S(1)} %get-tuple-element.15, s32[128]{0:T(128)S(1)} %bitcast.126), kind=kCustom, calls=%fused_computation.2 | custom fusion | bytes 2560 | tf_op jit(solution)/shard_map/scatter | solution.py:107
  82.1 0.7 copy.100
  82.8 9.2 %all-to-all-start = ((s32[32,1,6]{2,1,0:T(1,128)}), s32[32,1,6]{2,1,0:T(1,128)S(1)}, u32[]{:S(2)}, u32[]{:S(2)}) async-start(s32[32,1,6]{2,1,0:T(1,128)} %copy.100), calls=%async_computation | async-start | bytes 32768 | tf_op jit(solution)/shard_map/all_to_all | solution.py:111
  92.0 0.0 reduce-scatter.5.cloned.1.call-start
  92.1 0.2 fusion.33
  92.3 0.5 copy.114
  92.9 2.0 gather_fusion
  94.9 5.6 %all-gather.5.cloned.1.call-done = bf16[1,128,9,512]{3,2,0,1:T(8,128)(2,1)} async-done(((bf16[1,4,9,512]{3,2,0,1:T(8,128)(2,1)}), bf16[1,128,9,512]{3,2,0,1:T(8,128)(2,1)}) %all-gather.5.cloned.1.call-update) | async-done | bytes 1179664 | tf_op jit(solution)/shard_map/all_gather | solution.py:60
  100.5 2.3 gather_fusion.1
  102.8 2.2 convolution_convert_fusion
  105.0 0.2 slice.56
  105.2 0.3 slice.60
  105.5 0.3 slice.58
  105.8 1.5 copy.122
  107.3 0.3 copy.120
  107.6 76.8 %all-gather.7.cloned.1.call-done = bf16[1,3,512,512]{3,2,1,0:T(8,128)(2,1)} async-done(((bf16[1,3,16,512]{3,2,1,0:T(8,128)(2,1)}), bf16[1,3,512,512]{3,2,1,0:T(8,128)(2,1)}) %all-gather.7.cloned.1.call-update) | async-done | bytes 1572880 | tf_op jit(solution)/shard_map/all_gather | solution.py:59
  184.4 1.3 fusion.13
  185.7 0.2 reshape.180
  185.9 1.6 fusion.17
  187.5 0.8 copy.111
  188.3 0.6 copy-done.2
  188.9 0.4 fusion.15
  189.3 0.5 copy.110
  189.8 0.6 copy-done.1
  190.5 3.6 fusion
  194.0 0.1 add_divide_fusion
  194.1 1.1 add_convert_fusion
  195.3 0.3 slice.64
  195.6 0.3 slice.63
  195.9 0.2 slice.62
  196.1 0.2 copy-done.7
  196.4 0.7 fusion.10
  197.1 0.5 fusion.9
  197.6 0.3 fusion.8
  197.9 1.3 pad_maximum_fusion.1
  199.3 0.4 fusion.14
  199.7 1.8 fusion.16
  201.5 0.3 convolution_bitcast_fusion.2
  201.8 0.2 pad_maximum_fusion
  202.0 6.6 %fusion.3 = bf16[128,9,512]{2,1,0:T(8,128)(2,1)} fusion(f32[128,9,9]{1,2,0:T(8,128)S(1)} %copy.114, f32[128,9,512]{2,0,1:T(8,128)S(1)} %pad_maximum_fusion), kind=kOutput, calls=%fused_computation.10 | convolution fusion | flops 64290816 | bytes 3580416 | tf_op jit(solution)/shard_map/eba,ebc->eac/dot_general | solution.py:29
  208.6 0.4 broadcast_in_dim.5
  209.0 13.2 %scatter_fusion.1 = bf16[32,6,9,512]{3,2,1,0:T(8,128)(2,1)S(1)} fusion(bf16[32,6,9,512]{3,2,1,0:T(8,128)(2,1)S(1)} %broadcast_in_dim.5, s32[128]{0:T(128)S(1)} %get-tuple-element.15, bf16[128,9,512]{2,1,0:T(8,128)(2,1)} %fusion.3), kind=kCustom, calls=%fused_computation.3 | custom fusion | bytes 3539968 | tf_op jit(solution)/shard_map/scatter | solution.py:102
  222.2 2.9 copy.116
  225.1 5.7 %all-to-all-start.1 = ((bf16[32,6,9,512]{3,1,2,0:T(8,128)(2,1)}), bf16[32,6,9,512]{3,1,2,0:T(8,128)(2,1)S(1)}, u32[]{:S(2)}, u32[]{:S(2)}) async-start(bf16[32,6,9,512]{3,1,2,0:T(8,128)(2,1)} %copy.116), calls=%async_computation.2 | async-start | bytes 4718592 | tf_op jit(solution)/shard_map/all_to_all | solution.py:110
  230.8 0.5 broadcast.173
  231.3 0.7 reduce.3
  232.0 0.1 eq.56
  232.1 195.9 %reduce-scatter.5.cloned.1.call-done = bf16[3,16,512]{2,1,0:T(8,128)(2,1)} async-done(((bf16[3,512,512]{2,1,0:T(8,128)(2,1)}), bf16[3,16,512]{2,1,0:T(8,128)(2,1)}) %reduce-scatter.5.cloned.1.call-update) | async-done | bytes 49168 | tf_op jit(solution)/shard_map/reduce_scatter | solution.py:89
  428.0 25.2 %all-gather.1 = bf16[48,16,512]{2,1,0:T(8,128)(2,1)S(1)} all-gather(bf16[3,16,512]{2,1,0:T(8,128)(2,1)} %reduce-scatter.5.cloned.1.call-done), channel_id=3, replica_groups=mesh['grp'=16,'graph'=32] {'grp'}, dimensions={0}, use_global_device_ids=true | all-gather | bytes 835584 | tf_op jit(solution)/shard_map/all_gather | solution.py:92
  453.2 0.9 fusion.11
  454.1 0.7 copy.126
  454.8 1.1 copy.117
  455.9 2.6 copy.134
  458.4 2.7 copy.118
  461.1 1.4 convolution_bitcast_fusion.3
  (49 shorter events, 0.3 us)
Async XLA Ops:
  8.0 0.9 copy-start
  8.0 3.4 copy-start.11
  8.0 67.1 %copy-start.14 = (s32[1,128,1]{1,2,0:T(1,128)S(1)}, s32[1,128,1]{1,2,0:T(1,128)}, u32[]{:S(2)}) copy-start(s32[1,128,1]{1,2,0:T(1,128)} %param.13) | copy-start | bytes 1540
  8.0 67.6 %copy-start.15 = (s32[1,128]{1,0:T(1,128)S(1)}, s32[1,128]{1,0:T(1,128)}, u32[]{:S(2)}) copy-start(s32[1,128]{1,0:T(1,128)} %param.14) | copy-start | bytes 1540
  8.0 67.1 %reduce-scatter.3.cloned.1.call-start = ((), (), s32[]{:S(2)}) async-start(), calls=%async_computation.5 | async-start | bytes 835584 | tf_op jit(solution)/shard_map/reduce_scatter | solution.py:51
  10.0 82.0 %copy-start.10 = (f32[64,9,9]{0,2,1:T(8,128)S(1)}, f32[64,9,9]{0,2,1:T(8,128)}, u32[]{:S(2)}) copy-start(f32[64,9,9]{0,2,1:T(8,128)} %param.17) | copy-start | bytes 62212
  10.0 82.1 %copy-start.16 = (s32[1,128]{1,0:T(1,128)S(1)}, s32[1,128]{1,0:T(1,128)}, u32[]{:S(2)}) copy-start(s32[1,128]{1,0:T(1,128)} %param.16) | copy-start | bytes 1540
  11.4 81.4 %copy-start.12 = (bf16[1,4,9,512]{3,1,2,0:T(4,128)(2,1)S(1)}, bf16[1,4,9,512]{3,1,2,0:T(4,128)(2,1)}, u32[]{:S(2)}) copy-start(bf16[1,4,9,512]{3,1,2,0:T(4,128)(2,1)} %param.10) | copy-start | bytes 110596
  11.4 81.4 %copy-start.17 = (s32[1,128]{1,0:T(1,128)S(1)}, s32[1,128]{1,0:T(1,128)}, u32[]{:S(2)}) copy-start(s32[1,128]{1,0:T(1,128)} %param.15) | copy-start | bytes 1540
  11.4 89.1 %all-gather.5.cloned.1.call-start = ((), (), s32[]{:S(2)}) async-start(), calls=%async_computation.4 | async-start | bytes 2162688 | tf_op jit(solution)/shard_map/all_gather | solution.py:60
  12.1 172.3 %all-gather.7.cloned.1.call-start = ((), (), s32[]{:S(2)}) async-start(), calls=%async_computation.7 | async-start | bytes 1622016 | tf_op jit(solution)/shard_map/all_gather | solution.py:59
  82.8 142.3 %all-to-all-start = ((s32[32,1,6]{2,1,0:T(1,128)}), s32[32,1,6]{2,1,0:T(1,128)S(1)}, u32[]{:S(2)}, u32[]{:S(2)}) async-start(s32[32,1,6]{2,1,0:T(1,128)} %copy.100), calls=%async_computation | async-start | bytes 32768 | tf_op jit(solution)/shard_map/all_to_all | solution.py:111
  92.0 336.0 %reduce-scatter.5.cloned.1.call-start = ((), (), s32[]{:S(2)}) async-start(), calls=%async_computation.6 | async-start | bytes 1622016 | tf_op jit(solution)/shard_map/reduce_scatter | solution.py:89
  107.3 78.6 %copy-start.6 = (bf16[128,5,512]{0,2,1:T(8,128)(2,1)S(1)}, bf16[128,5,512]{0,2,1:T(8,128)(2,1)}, u32[]{:S(2)}) copy-start(bf16[128,5,512]{0,2,1:T(8,128)(2,1)} %copy.122) | copy-start | bytes 1966084
  187.5 1.4 copy-start.2
  188.9 1.6 copy-start.1
  195.3 1.1 copy-start.7
  195.6 1.9 copy-start.5
  195.9 1.6 copy-start.3
  196.4 1.2 copy-start.8
  197.9 1.3 copy-start.4
  199.3 2.2 copy-start.9
  225.1 228.2 %copy-start.13 = (s32[16,32]{1,0:T(8,128)S(1)}, s32[16,32]{1,0:T(8,128)}, u32[]{:S(2)}) copy-start(s32[16,32]{1,0:T(8,128)} %param.12) | copy-start | bytes 6148
  225.1 229.7 %all-to-all-start.1 = ((bf16[32,6,9,512]{3,1,2,0:T(8,128)(2,1)}), bf16[32,6,9,512]{3,1,2,0:T(8,128)(2,1)S(1)}, u32[]{:S(2)}, u32[]{:S(2)}) async-start(bf16[32,6,9,512]{3,1,2,0:T(8,128)(2,1)} %copy.116), calls=%async_computation.2 | async-start | bytes 4718592 | tf_op jit(solution)/shard_map/all_to_all | solution.py:110
Sparse Core Ops, SparseCore 0:
  11.7 63.4 reduce-scatter.2
Sparse Core Ops, SparseCore 1:
  15.6 84.8 all-gather.4
  104.0 80.3 all-gather.6
  199.3 228.6 reduce-scatter.4
where the time goes:
time: 471 us; the launch traced here: 470 us
  waiting for transfers between devices  341 us (72%)
  local copies, waits for them, and re-layouts  45.3 us (10%)
  blocking collectives  25.2 us (5%)
  matrix products  23.1 us (5%)
  between operations  16.2 us (3%)
  starting transfers between devices  15.1 us (3%)
    reduce_scatter x1, waiting for transfers between devices, shards(): lax.psum_scatter(jnp.stack(weight_terms).astype(jnp.bfloat16), 'graph', s...  196 us
    all_gather x1, waiting for transfers between devices, shards(): lax.all_gather(mixed_rows[0].astype(jnp.bfloat16), 'graph', axis=1, tiled...  76.8 us
    reduce_scatter x1, waiting for transfers between devices, shards(): lax.psum_scatter(jnp.einsum('sk,klab->slab', narrow_shares, expert_weight...  63 us
    all_gather x1, blocking collectives, shards(): lax.all_gather(weight_rows[None].astype(jnp.bfloat16), 'grp', axis=0, til...  25.2 us
    scatter x2, local copies, waits for them, and re-layouts, shards(): outgoing = jnp.zeros((peer_count, capacity, 9, channels), jnp.bfloat16).a...  16.1 us
    dot_general x3, matrix products, rotate(): jnp.einsum(form, rotations, values.astype(jnp.float32), precision=precise)  12.3 us
  transfers between devices with their start and end apart: 6, of which 4 were waited for; matrix products, arithmetic and copies ran while one was open for 13% of the time, Pallas kernels for 0%

commit v1 on v0

v1 whole, which is shorter than its diff:
```python
import jax
import jax.numpy as jnp
from jax import lax
from jax.experimental import pallas as pl
from jax.experimental.pallas import tpu as pltpu
from jax.sharding import PartitionSpec as P

F32, BF16, I32 = jnp.float32, jnp.bfloat16, jnp.int32
NX, NZ, NY = 4, 8, 8
SPANS = ((0, 1), (1, 4), (4, 9))
DEGREE = (0, 1, 1, 1, 2, 2, 2, 2, 2)
MESH = pl.DeviceIdType.MESH
NN = (((1,), (0,)), ((), ()))
NT = (((1,), (1,)), ((), ()))

(PH_CORE, PH_Y, PH_YX, PH_ATX, PH_ATR, PH_ATL, PH_COX, PH_COZ, PH_MZ, PH_MC,
 PH_GZ, PH_GX, PH_SZ, PH_SYX, PH_FW, PH_END) = range(16)
NEAR = (-2, -1, 0, 1, 2)
ENTRY = {}
for _opening, _closing in SPANS:
    for _i in range(_opening, _closing):
        for _b in range(_opening, _closing):
            ENTRY[_i, _b] = len(ENTRY)


def dot(a, b, dims=NN):
    return lax.dot_general(a, b, dims, preferred_element_type=F32)


def one_hot(test):
    return jnp.where(test, 1.0, 0.0).astype(BF16)


def grid_of(rows, columns):
    shape = (rows, columns)
    return lax.broadcasted_iota(I32, shape, 0), lax.broadcasted_iota(I32, shape, 1)


def split48(index):
    block = jnp.where(index >= 48, 1, 0) + jnp.where(index >= 96, 1, 0) + jnp.where(index >= 144, 1, 0)
    return block, index - 48 * block


def kernel(
    coef, w_hbm, at_hbm, co_hbm, owner_hbm, slot_hbm, tslot_hbm, turn_hbm, rt_hbm,
    ga_ref, ge_ref,
    w_own, w_sib, at_in, co_in, index_in, rt_in, rt35,
    ybuf, yrecv, yxbuf, yxrecv, mx, mzbuf, wc, mc,
    at48, atx, a_ref, co80, cox, cobuf, corecv,
    expand, fold, spread, perm, unperm, order, gather16, same, rot2,
    hs, cs, hh, ch, grads_at, turns, oh, u_ref, g_acc, gbuf, grecv, gxbuf, gxrecv,
    sgt, sgbuf, sgrecv, sg4, sgx, forwarded, endbuf, endrecv,
    load_sem, send_sem, recv_sem,
):
    grp, graph = lax.axis_index("grp"), lax.axis_index("graph")
    y, core = lax.div(grp, 2), lax.rem(grp, 2)
    x, z = lax.div(graph, NZ), lax.rem(graph, NZ)

    def device(dy=None, dx=None, dz=None, other=False):
        along = y if dy is None else lax.rem(y + dy + NY, NY)
        across = x if dx is None else lax.rem(x + dx, NX)
        up = z if dz is None else lax.rem(z + dz, NZ)
        return {"grp": along * 2 + (1 - core if other else core), "graph": across * NZ + up}

    def remote(phase, slot, source, target, place):
        return pltpu.make_async_remote_copy(
            src_ref=source, dst_ref=target, send_sem=send_sem.at[phase, slot],
            recv_sem=recv_sem.at[phase, slot], device_id=place, device_id_type=MESH,
        )

    def each(count, body):
        def step(d, carry):
            body(d)
            return carry

        lax.fori_loop(1, count, step, 0)

    def arrived(phase, slot, ref):
        pltpu.make_async_copy(ref, ref, recv_sem.at[phase, slot]).wait()

    def left(phase, slot, ref):
        pltpu.make_async_copy(ref, ref, send_sem.at[phase, slot]).wait()

    loads = [
        pltpu.make_async_copy(source, target, load_sem.at[k])
        for k, (source, target) in enumerate((
            (w_hbm, w_own), (at_hbm, at_in), (co_hbm, co_in), (owner_hbm, index_in.at[0]),
            (slot_hbm, index_in.at[1]), (tslot_hbm, index_in.at[2]), (turn_hbm, index_in.at[3]),
            (rt_hbm, rt_in)))
    ]
    for load in loads:
        load.start()

    barrier = pltpu.get_barrier_semaphore()

    def greet(place):
        pl.semaphore_signal(barrier, inc=1, device_id=place, device_id_type=MESH)

    greet(device(other=True))
    for dy in NEAR:
        if dy:
            greet(device(dy=dy))
        each(NX, lambda d: greet(device(dy=dy, dx=d)))
    each(NZ, lambda d: greet(device(dz=d)))

    row, column = grid_of(144, 192)
    block, within = split48(column)
    order[...] = one_hot(
        ((within >> 2) == (row >> 4)) & (((row >> 2) & 3) == block) & ((within & 3) == (row & 3)))
    row, column = grid_of(16, 192)
    block, within = split48(column)
    gather16[...] = one_hot(row == block * 4 + (within & 3))
    row, column = grid_of(192, 16)
    block, within = split48(row)
    expand[...] = one_hot(column == block * 4 + (within & 3))
    row, column = grid_of(192, 256)
    block, within = split48(row)
    same[...] = jnp.where((within >> 2) == (column >> 4), 1.0, 0.0)
    for t in range(NZ):
        row, column = grid_of(128, 256)
        spread[t] = one_hot(((row >> 4) == t) & ((row & 15) == (column & 15)))
        row, column = grid_of(256, 128)
        fold[t] = one_hot(((column >> 4) == t) & ((row & 15) == (column & 15)))
        for l in range(3):
            row, column = grid_of(128, 128)
            perm[l, :, t * 128:(t + 1) * 128] = one_hot(
                ((row >> 4) == t) & ((column >> 4) == l) & ((row & 15) == (column & 15)))
            unperm[t, :, l * 128:(l + 1) * 128] = one_hot(
                ((column >> 4) == t) & ((row >> 4) == l) & ((row & 15) == (column & 15)))

    for load in loads:
        load.wait()

    for b in range(9):
        co80[0, b * 4:b * 4 + 4, :] = co_in[b].astype(F32)
        at48[0, b * 4:b * 4 + 4, :] = at_in[b].astype(F32)
    at48[0, 36:48, :] = jnp.zeros((12, 512), F32)
    co80[0, 36:48, :] = jnp.zeros((12, 512), F32)

    def place(owner, slot):
        return (owner & 7) * 16 + (owner >> 3) * 4 + slot

    row = lax.broadcasted_iota(I32, (16, 128), 0)
    codes = jnp.where(row == 0, place(index_in[0], index_in[1]), 0)
    codes = jnp.where(row == 1, place(graph, index_in[2]), codes)
    codes = jnp.where(row == 2, index_in[3], codes).astype(F32).astype(BF16)
    for xb in range(NX):
        at = slice(xb * 128, (xb + 1) * 128)
        atx_out = at48[0, :, at].astype(BF16)
        cox_out = co80[0, :, at].astype(BF16)
        atx[NX, xb] = atx_out
        cox[NX + xb, 0:48, :] = cox_out
        cox[NX + xb, 48:64, :] = codes

    pl.semaphore_wait(barrier, 1 + 4 + 5 * (NX - 1) + (NZ - 1))

    core_copy = remote(PH_CORE, 0, w_own, w_sib, device(other=True))
    core_copy.start()
    each(NX, lambda d: remote(PH_ATX, 0, atx.at[NX], atx.at[x], device(dx=d)).start())
    each(NX, lambda d: remote(
        PH_COX, 0, cox.at[NX + lax.rem(x + d, NX)], cox.at[x], device(dx=d)).start())
    atx[x] = atx[NX]
    cox[x] = cox[NX + x]

    core_copy.wait_recv()

    def share(dy, expert):
        return coef[lax.rem(y + dy + NY, NY) * 2 + core, expert].astype(F32) * (1.0 / 1024.0)

    own_first, other_first = grp * 2, (y * 2 + 1 - core) * 2

    def partial_of(dy, xb):
        at = slice(xb * 128, (xb + 1) * 128)
        total = None
        for ref, first in ((w_own, own_first), (w_sib, other_first)):
            for e in range(2):
                term = share(dy, first + e) * ref[e, :, :, at].astype(F32)
                total = term if total is None else total + term
        return total

    steps = ((0, -4, -2), (1, 3, 1), (2, -3, -1))
    for slot, dy, hop in steps:
        for xb in range(NX):
            ybuf[slot, xb] = partial_of(dy, xb).astype(BF16)
        remote(PH_Y, slot, ybuf.at[slot], yrecv.at[slot], device(dy=hop)).start()

    def yx_send(k):
        dy = NEAR[k]
        if dy:
            remote(PH_YX, k, yxbuf.at[k, x], yxrecv.at[k, x], device(dy=dy)).start()
        else:
            yxrecv[k, x] = yxbuf[k, x]
        each(NX, lambda d: remote(
            PH_YX, k, yxbuf.at[k, lax.rem(x + d, NX)], yxrecv.at[k, x], device(dy=dy, dx=d)).start())

    for k in (1, 3, 2):
        for xb in range(NX):
            yxbuf[k, xb] = partial_of(NEAR[k], xb).astype(BF16)
        yx_send(k)

    arrived(PH_ATX, 0, atx.at[pl.ds(0, NX - 1)])
    for xb in range(NX):
        stacked = jnp.concatenate([atx[s, xb] for s in range(NX)], axis=0)
        a_ref[z, :, :, xb * 128:(xb + 1) * 128] = dot(order[...], stacked).astype(BF16).reshape(9, 16, 128)

    def right_copy(s):
        slot = lax.rem(z - s + NZ, NZ)
        return remote(PH_ATR, s, a_ref.at[slot], a_ref.at[slot], device(dz=1))

    def left_copy(s):
        slot = lax.rem(z + s, NZ)
        return remote(PH_ATL, s, a_ref.at[slot], a_ref.at[slot], device(dz=NZ - 1))

    arrived(PH_COX, 0, cox.at[pl.ds(0, NX - 1)])
    stacked = jnp.concatenate([cox[s, 0:48] for s in range(NX)], axis=0)
    for t in range(NZ):
        wide = (dot(stacked, spread[t]) * same[...]).astype(BF16)
        packed = dot(gather16[...], wide).astype(BF16)
        cobuf[t, 0] = packed[:, 0:128]
        cobuf[t, 1] = packed[:, 128:256]
        for s in range(NX):
            cobuf[t, 2 + s] = cox[s, 48:64]
    each(NZ, lambda d: remote(
        PH_COZ, 0, cobuf.at[lax.rem(z + d, NZ)], corecv.at[z], device(dz=d)).start())
    corecv[z] = cobuf[z]
    right_copy(0).start()
    left_copy(0).start()

    for slot in range(3):
        arrived(PH_Y, slot, yrecv.at[slot])
    for xb in range(NX):
        yxbuf[0, xb] = (partial_of(-2, xb) + yrecv[0, xb].astype(F32) + yrecv[2, xb].astype(F32)).astype(BF16)
    yx_send(0)
    for xb in range(NX):
        yxbuf[4, xb] = (partial_of(2, xb) + yrecv[1, xb].astype(F32)).astype(BF16)
    yx_send(4)

    for i in range(9):
        opening, closing = SPANS[DEGREE[i]]
        first = ENTRY[i, opening]
        rt35[first:first + closing - opening, :] = rt_in[i, opening:closing, :]
    rt35[35:40, :] = jnp.zeros((5, 64), F32)
    table = rt35[...]
    high = table.astype(BF16)
    rot2[:, 0:64] = high
    rot2[:, 64:128] = (table - high.astype(F32)).astype(BF16)

    arrived(PH_COZ, 0, corecv.at[pl.ds(0, NZ - 1)])
    for half in range(2):
        tall = jnp.transpose(corecv[:, half].reshape(128, 128).astype(F32)).astype(BF16)
        rows = 128 if half == 0 else 16
        cs[half * 128:half * 128 + rows, :] = tall[0:rows]

    def turned(entries, values, opening, closing, i):
        total = entries[i, opening] * values(opening)
        for b in range(opening + 1, closing):
            total = total + entries[i, b] * values(b)
        return total

    def entries_of(t, at):
        return {key: turns[t, k:k + 1, at] for key, k in ENTRY.items()}

    def prepare(t, carry):
        lanes = lax.broadcasted_iota(I32, (128, 128), 0).astype(F32)
        folded = (lax.broadcasted_iota(I32, (128, 128), 0) & 63).astype(F32)
        for q in range(NX):
            at = slice(q * 128, (q + 1) * 128)
            codes = corecv[t, 2 + q].astype(F32)
            oh[t, :, at] = one_hot(lanes == codes[0:1])
            oh[NZ, :, at] = one_hot(lanes == codes[1:2])
            oh[NZ + 1, :, at] = one_hot(folded == codes[2:3])
        ch[...] = dot(cs[...], oh[NZ])
        turns[t] = dot(rot2[...], oh[NZ + 1])
        for q in range(NX):
            at = slice(q * 128, (q + 1) * 128)
            entries = entries_of(t, at)
            for opening, closing in SPANS:
                for i in range(opening, closing):
                    grads_at[t, i * 16:(i + 1) * 16, at] = turned(
                        entries, lambda b: ch[b * 16:(b + 1) * 16, at], opening, closing, i)
        return carry

    def pass_on(s):
        right_copy(s - 1).wait_recv()
        right_copy(s).start()
        left_copy(s - 1).wait_recv()
        if s < 3:
            left_copy(s).start()

    pass_on(1)
    lax.fori_loop(0, 3, prepare, 0)
    pass_on(2)
    lax.fori_loop(3, 5, prepare, 0)

    for k, dy in enumerate(NEAR):
        arrived(PH_YX, k, yxrecv.at[k] if dy else yxrecv.at[k, pl.ds(0, NX - 1)])
    packed = jnp.zeros((64, 1024), F32)
    for l in range(3):
        for s in range(NX):
            total = yxrecv[0, s, l].astype(F32)
            for k in range(1, 5):
                total = total + yxrecv[k, s, l].astype(F32)
            mx[s, l] = total.astype(BF16)
        packed = packed + dot(mx[:, l].reshape(64, 128), perm[l])
    packed = packed.astype(BF16)
    for t in range(NZ):
        mzbuf[t] = packed[:, t * 128:(t + 1) * 128].reshape(NX, 16, 128)
    each(NZ, lambda d: remote(
        PH_MZ, 0, mzbuf.at[lax.rem(z + d, NZ)], wc.at[z], device(dz=d)).start())
    wc[z] = mzbuf[z]
    mc[z] = mx[...]
    pass_on(3)
    lax.fori_loop(5, 8, prepare, 0)
    right_copy(3).wait_recv()
    arrived(PH_MZ, 0, wc.at[pl.ds(0, NZ - 1)])
    each(NZ, lambda d: remote(PH_MC, 0, mx, mc.at[z], device(dz=d)).start())

    columns16 = jnp.concatenate(
        [jnp.concatenate([wc[t, s] for t in range(NZ)], axis=0) for s in range(NX)], axis=0)
    flipped = jnp.transpose(columns16.astype(F32)).astype(BF16)
    for b in range(9):
        l = DEGREE[b]
        hs[b * 16:(b + 1) * 16, :] = dot(
            flipped[l * 16:(l + 1) * 16], a_ref[:, b].reshape(128, 512), NT).astype(BF16)

    g_acc[...] = jnp.zeros(g_acc.shape, F32)

    def edges(t, carry):
        hh[...] = dot(hs[...], oh[t])
        for q in range(NX):
            at = slice(q * 128, (q + 1) * 128)
            entries = entries_of(t, at)
            grads, inner, gate = [], None, None
            for opening, closing in SPANS:
                for i in range(opening, closing):
                    hidden = turned(entries, lambda b: hh[b * 16:(b + 1) * 16, at], opening, closing, i)
                    grad = grads_at[t, i * 16:(i + 1) * 16, at]
                    if i == 0:
                        gate = jax.nn.sigmoid(hidden)
                    inner = grad * hidden if inner is None else inner + grad * hidden
                    grads.append(grad * gate)
            grads[0] = grads[0] + inner * gate * (1.0 - gate)
            for opening, closing in SPANS:
                for b in range(opening, closing):
                    total = entries[opening, b] * grads[opening]
                    for i in range(opening + 1, closing):
                        total = total + entries[i, b] * grads[i]
                    u_ref[b * 16:(b + 1) * 16, at] = total.astype(BF16)
        g_acc[...] += dot(u_ref[...], oh[t], NT)
        return carry

    lax.fori_loop(0, NZ, edges, 0)

    sums = g_acc[...]
    narrow = sums.astype(BF16)
    sgt[48:128, :] = jnp.zeros((80, 512), F32)
    for l, (opening, closing) in enumerate(SPANS):
        total = jnp.zeros((16, 512), F32)
        for b in range(opening, closing):
            total = total + dot(narrow[b * 16:(b + 1) * 16], a_ref[:, b].reshape(128, 512))
        sgt[l * 16:(l + 1) * 16, :] = total
    tall = jnp.transpose(sgt[...]).astype(BF16)
    for t in range(NZ):
        for s in range(NX):
            first = s * 128 + t * 16
            sgbuf[t, s] = tall[first:first + 16]
    each(NZ, lambda d: remote(
        PH_SZ, 0, sgbuf.at[lax.rem(z + d, NZ)], sgrecv.at[z], device(dz=d)).start())
    sgrecv[z] = sgbuf[z]
    turned_sums = jnp.transpose(
        jnp.concatenate([sums, jnp.zeros((112, 128), F32)], axis=0)).astype(BF16)
    for t in range(NZ):
        gbuf[t] = turned_sums[t * 16:(t + 1) * 16]
    each(NZ, lambda d: remote(
        PH_GZ, 0, gbuf.at[lax.rem(z + d, NZ)], grecv.at[z], device(dz=d)).start())
    grecv[z] = gbuf[z]

    arrived(PH_SZ, 0, sgrecv.at[pl.ds(0, NZ - 1)])
    rows = dot(sgrecv[0].reshape(64, 128), unperm[0])
    for t in range(1, NZ):
        rows = rows + dot(sgrecv[t].reshape(64, 128), unperm[t])
    for s in range(NX):
        for l in range(3):
            sg4[s, l] = rows[s * 16:(s + 1) * 16, l * 128:(l + 1) * 128].astype(BF16)

    for k in (0, 4, 1, 3, 2):
        dy = NEAR[k]
        if dy:
            remote(PH_SYX, k, sg4.at[x], sgx.at[k, x], device(dy=dy)).start()
        else:
            sgx[k, x] = sg4[x]
        each(NX, lambda d: remote(
            PH_SYX, k, sg4.at[lax.rem(x + d, NX)], sgx.at[k, x], device(dy=dy, dx=d)).start())

    arrived(PH_GZ, 0, grecv.at[pl.ds(0, NZ - 1)])
    held = jnp.zeros((192, 128), F32)
    for t in range(NZ):
        wide = (dot(expand[...], grecv[t]) * same[...]).astype(BF16)
        held = held + dot(wide, fold[t])

    arrived(PH_SYX, 0, sgx.at[0])
    arrived(PH_SYX, 4, sgx.at[4])
    onward = ((0, 0, -2), (1, 4, 1), (2, 0, -1))
    for slot, k, hop in onward:
        remote(PH_FW, slot, sgx.at[k], forwarded.at[slot], device(dy=hop)).start()

    arrived(PH_MC, 0, mc.at[pl.ds(0, NZ - 1)])
    coefficient = split48(lax.broadcasted_iota(I32, (192, 128), 0))[1] >> 2
    parts = jnp.zeros((192, 512), F32)
    for l, (opening, closing) in enumerate(SPANS):
        inside = (coefficient >= opening) & (coefficient < closing)
        maps = jnp.concatenate(
            [jnp.concatenate([mc[t, s, l] for t in range(NZ)], axis=0) for s in range(NX)], axis=0)
        parts = parts + dot(jnp.where(inside, held, 0.0).astype(BF16), maps, NT)
    for s in range(NX):
        gxbuf[s] = parts[s * 48:(s + 1) * 48].astype(BF16)
    each(NX, lambda d: remote(
        PH_GX, 0, gxbuf.at[lax.rem(x + d, NX)], gxrecv.at[d], device(dx=d)).start())
    gxrecv[0] = gxbuf[x]
    for k in (1, 2, 3):
        arrived(PH_SYX, k, sgx.at[k] if NEAR[k] else sgx.at[k, pl.ds(0, NX - 1)])
    arrived(PH_GX, 0, gxrecv.at[pl.ds(0, NX - 1)])
    total = gxrecv[0].astype(F32)
    for s in range(1, NX):
        total = total + gxrecv[s].astype(F32)
    for b in range(9):
        ga_ref[b] = total[b * 4:b * 4 + 4]

    for slot in range(3):
        arrived(PH_FW, slot, forwarded.at[slot])

    def expert_sum(expert, s):
        total = None
        for k, dy in enumerate(NEAR):
            term = share(-dy, expert) * sgx[k, s].astype(F32)
            total = term if total is None else total + term
        for slot, dy in ((0, 4), (1, -3), (2, 3)):
            total = total + share(dy, expert) * forwarded[slot, s].astype(F32)
        return total

    for e in range(2):
        for s in range(NX):
            endbuf[e, s] = expert_sum(other_first + e, s).astype(BF16)
    end_copy = remote(PH_END, 0, endbuf, endrecv, device(other=True))
    end_copy.start()
    for e in range(2):
        for s in range(NX):
            ge_ref[e, :, :, s * 128:(s + 1) * 128] = expert_sum(own_first + e, s)
    end_copy.wait_recv()
    for e in range(2):
        for s in range(NX):
            ge_ref[e, :, :, s * 128:(s + 1) * 128] += endrecv[e, s].astype(F32)

    core_copy.wait_send()
    end_copy.wait_send()
    for s in range(4):
        right_copy(s).wait_send()
    for s in range(3):
        left_copy(s).wait_send()
    for slot in range(3):
        left(PH_Y, slot, ybuf.at[slot])
        left(PH_FW, slot, forwarded.at[slot])
    for k, dy in enumerate(NEAR):
        left(PH_YX, k, yxbuf.at[k] if dy else yxbuf.at[k, pl.ds(0, NX - 1)])
        left(PH_SYX, k, sg4 if dy else sg4.at[pl.ds(0, NX - 1)])
    left(PH_ATX, 0, atx.at[pl.ds(0, NX - 1)])
    left(PH_COX, 0, cox.at[pl.ds(0, NX - 1)])
    left(PH_GX, 0, gxbuf.at[pl.ds(0, NX - 1)])
    left(PH_COZ, 0, cobuf.at[pl.ds(0, NZ - 1)])
    left(PH_MZ, 0, mzbuf.at[pl.ds(0, NZ - 1)])
    left(PH_MC, 0, mc.at[pl.ds(0, NZ - 1)])
    left(PH_SZ, 0, sgbuf.at[pl.ds(0, NZ - 1)])
    left(PH_GZ, 0, gbuf.at[pl.ds(0, NZ - 1)])


def shards(
    atoms, cotangent, expert_weights, coefficients, src_owner, src_slot, tgt_slot, rot_index, rot_table
):
    hbm = pl.BlockSpec(memory_space=pltpu.HBM)
    vmem = pl.BlockSpec(memory_space=pltpu.VMEM)
    smem = pl.BlockSpec(memory_space=pltpu.SMEM)

    def b16(*shape):
        return pltpu.VMEM(shape, BF16)

    def f32(*shape):
        return pltpu.VMEM(shape, F32)

    grad_atoms, grad_experts = pl.pallas_call(
        kernel,
        out_shape=(
            jax.ShapeDtypeStruct((9, 4, 512), F32),
            jax.ShapeDtypeStruct((2, 3, 16, 512), F32),
        ),
        in_specs=[smem] + [hbm] * 8,
        out_specs=(vmem, vmem),
        scratch_shapes=[
            b16(2, 3, 16, 512),
            b16(2, 3, 16, 512),
            b16(9, 4, 512),
            b16(9, 4, 512),
            pltpu.VMEM((4, 1, 128), I32),
            f32(9, 9, 64),
            f32(40, 64),
            b16(3, NX, 3, 16, 128),
            b16(3, NX, 3, 16, 128),
            b16(5, NX, 3, 16, 128),
            b16(5, NX, 3, 16, 128),
            b16(NX, 3, 16, 128),
            b16(NZ, NX, 16, 128),
            b16(NZ, NX, 16, 128),
            b16(NZ, NX, 3, 16, 128),
            f32(1, 48, 512),
            b16(NX + 1, NX, 48, 128),
            b16(NZ, 9, 16, 512),
            f32(1, 48, 512),
            b16(2 * NX, 64, 128),
            b16(NZ, 6, 16, 128),
            b16(NZ, 6, 16, 128),
            b16(192, 16),
            b16(NZ, 256, 128),
            b16(NZ, 128, 256),
            b16(3, 128, 1024),
            b16(NZ, 128, 384),
            b16(144, 192),
            b16(16, 192),
            f32(192, 256),
            b16(40, 128),
            b16(144, 128),
            b16(144, 128),
            f32(144, 512),
            f32(144, 512),
            f32(NZ, 144, 512),
            f32(NZ, 40, 512),
            b16(NZ + 2, 128, 512),
            b16(144, 512),
            f32(144, 128),
            b16(NZ, 16, 256),
            b16(NZ, 16, 256),
            b16(NX, 48, 512),
            b16(NX, 48, 512),
            f32(128, 512),
            b16(NZ, NX, 16, 128),
            b16(NZ, NX, 16, 128),
            b16(NX, 3, 16, 128),
            b16(5, NX, 3, 16, 128),
            b16(3, NX, 3, 16, 128),
            b16(2, NX, 3, 16, 128),
            b16(2, NX, 3, 16, 128),
            pltpu.SemaphoreType.DMA((8,)),
            pltpu.SemaphoreType.DMA((16, 5)),
            pltpu.SemaphoreType.DMA((16, 5)),
        ],
        compiler_params=pltpu.CompilerParams(
            collective_id=0, has_side_effects=True, vmem_limit_bytes=60 * 1024 * 1024
        ),
        cost_estimate=pl.CostEstimate(
            flops=2_000_000_000, bytes_accessed=1_000_000, transcendentals=65536
        ),
    )(
        coefficients, expert_weights, atoms[0].transpose(1, 0, 2), cotangent[0].transpose(1, 0, 2),
        src_owner.reshape(1, -1), src_slot, tgt_slot, rot_index, rot_table.transpose(1, 2, 0),
    )
    return grad_atoms.transpose(1, 0, 2)[None], grad_experts


def solution(mesh):
    placed = (
        P("grp", "graph", None, None),
        P("grp", "graph", None, None),
        P("grp", None, "graph", None),
        P(),
        P("grp", "graph", None),
        P("grp", "graph"),
        P("grp", "graph"),
        P("grp", "graph"),
        P(),
    )
    return jax.shard_map(
        shards,
        mesh=mesh,
        in_specs=placed,
        out_specs=(P("grp", "graph", None, None), P("grp", None, "graph", None)),
        check_vma=False,
    )
```

time: 471 us -> 79 us (0.17)
  waiting for transfers between devices: 341 us -> 0 us
  Pallas kernels: 0 us -> 75 us
  local copies, waits for them, and re-layouts: 45.3 us -> 3.14 us
  blocking collectives: 25.2 us -> 0 us
  matrix products: 23.1 us -> 0 us
  between operations: 16.2 us -> 0.64 us
  starting transfers between devices: 15.1 us -> 0 us
    reduce_scatter x2 -> x0, waiting for transfers between devices: 259 us -> none  [the longest x1 196 us: shards(): lax.psum_scatter(jnp.stack(weight_terms).astype(jnp.bfloat16), 'graph', s...]
    all_gather x2 -> x0, waiting for transfers between devices: 82.4 us -> none  [the longest x1 76.8 us: shards(): lax.all_gather(mixed_rows[0].astype(jnp.bfloat16), 'graph', axis=1, tiled...]
    pallas_call x0 -> x1, Pallas kernels: none -> 75 us  [shards(): pl.pallas_call(kernel, out_shape=(jax.ShapeDtypeStruct((9, 4, 512), F32),...]
    all_gather x1 -> x0, blocking collectives: 25.2 us -> none  [shards(): lax.all_gather(weight_rows[None].astype(jnp.bfloat16), 'grp', axis=0, til...]
    dot_general x16 -> x0, matrix products: 23.1 us -> none  [the longest x3 12.3 us: rotate(): jnp.einsum(form, rotations, values.astype(jnp.float32), precision=precise)]
    scatter x3 -> x0, local copies, waits for them, and re-layouts: 22.5 us -> none  [the longest x2 16.1 us: shards(): outgoing = jnp.zeros((peer_count, capacity, 9, channels), jnp.bfloat16).a...]
    all_to_all x2 -> x0, starting transfers between devices: 14.9 us -> none  [the longest x1 9.2 us: shards(): lax.all_to_all(slot_ids, 'graph', split_axis=0, concat_axis=0, tiled=True)]
  transfers between devices with their start and end apart: 6 -> 0, of which waited for: 4 -> 0; matrix products, arithmetic and copies ran while one was open for 13% -> 0% of each run, Pallas kernels for 0% -> 0%
where the time goes in v1:
time: 79 us; the launch traced here: 78.8 us
  Pallas kernels  75 us (95%)
  local copies, waits for them, and re-layouts  3.14 us (4%)
    pallas_call x1, Pallas kernels, shards(): pl.pallas_call(kernel, out_shape=(jax.ShapeDtypeStruct((9, 4, 512), F32),...  75 us
    unnamed x2, local copies, waits for them, and re-layouts  3.14 us

profile of v1, /device:TPU:1, one launch (start us, length us, event | category | flops | bytes accessed | tf_op | source)
XLA Modules:
  0.0 78.8 jit_solution(4640553756308322261)
XLA Ops:
  0.6 75.0 %shard_map.104 = (f32[9,4,512]{2,1,0:T(4,128)}, f32[2,3,16,512]{3,2,1,0:T(8,128)}) custom-call(s32[16,32]{1,0:T(8,128)} %coef.1, bf16[2,3,16,512]{3,2,1,0:T(8,128)(2,1)} %w_hbm.1, bf16[9,4,512]{2,1,0:T(4,128)(2,1)} %bitcast.13, bf16[9,4,512]{2,1,0:T(4,128)(2,1)} %bitcast.14, s32[1,128]{1,0:T(1,128)} %bitcast.15, s32[1,128]{1,0:T(1,128)} %slot_hbm.1, ...), custom_call_target="tpu_custom_call" | custom-call | flops 2000000000 | bytes 1000000 | tf_op jit(solution)/shard_map/pallas_call | solution.py:489
  75.7 1.5 %copy.13 = f32[1,4,9,512]{3,1,2,0:T(4,128)} copy(f32[1,4,9,512]{3,1,2,0:T(4,128)} %bitcast.11) | data formatting | bytes 147456
  77.2 1.6 %copy.14 = f32[2,3,16,512]{3,2,1,0:T(8,128)} copy(f32[2,3,16,512]{3,2,1,0:T(8,128)} %get-tuple-element.9) | data formatting | bytes 393216

commit v2 on v1

v2 whole, which is shorter than its diff:
```python
import jax
import jax.numpy as jnp
from jax import lax
from jax.experimental import pallas as pl
from jax.experimental.pallas import tpu as pltpu
from jax.sharding import PartitionSpec as P

F32, BF16, I32 = jnp.float32, jnp.bfloat16, jnp.int32
NX, NZ, NY = 4, 8, 8
SPANS = ((0, 1), (1, 4), (4, 9))
DEGREE = (0, 1, 1, 1, 2, 2, 2, 2, 2)
MESH = pl.DeviceIdType.MESH
NN = (((1,), (0,)), ((), ()))
NT = (((1,), (1,)), ((), ()))

(PH_CORE, PH_Y, PH_YX, PH_ATX, PH_ATR, PH_ATL, PH_COX, PH_COZ, PH_MZ, PH_MC,
 PH_GZ, PH_GX, PH_SZ, PH_SYX, PH_FW, PH_END, PH_MCL) = range(17)
NEAR = (-2, -1, 0, 1, 2)
ENTRY = {}
for _opening, _closing in SPANS:
    for _i in range(_opening, _closing):
        for _b in range(_opening, _closing):
            ENTRY[_i, _b] = len(ENTRY)


def dot(a, b, dims=NN):
    return lax.dot_general(a, b, dims, preferred_element_type=F32)


def one_hot(test):
    return jnp.where(test, 1.0, 0.0).astype(BF16)


def grid_of(rows, columns):
    shape = (rows, columns)
    return lax.broadcasted_iota(I32, shape, 0), lax.broadcasted_iota(I32, shape, 1)


def split48(index):
    block = jnp.where(index >= 48, 1, 0) + jnp.where(index >= 96, 1, 0) + jnp.where(index >= 144, 1, 0)
    return block, index - 48 * block


def kernel(
    coef, w_hbm, at_hbm, co_hbm, owner_hbm, slot_hbm, tslot_hbm, turn_hbm, rt_hbm,
    ga_ref, ge_ref,
    w_own, w_sib, at_in, co_in, index_in, rt_in, rt35,
    ybuf, yrecv, yxbuf, yxrecv, mx, mzbuf, wc, mc, maps16,
    at48, atx, a_ref, co80, cox, cobuf, corecv,
    expand, fold, spread, perm, unperm, order, gather16, same, rot2,
    hs, cs, hh, ch, grads_at, turns, oh, u_ref, g_acc, narrow, gbuf, grecv, gxbuf, gxrecv,
    sgt, sgbuf, sgrecv, sg4, sgx, forwarded, endbuf, endrecv,
    load_sem, send_sem, recv_sem,
):
    grp, graph = lax.axis_index("grp"), lax.axis_index("graph")
    y, core = lax.div(grp, 2), lax.rem(grp, 2)
    x, z = lax.div(graph, NZ), lax.rem(graph, NZ)

    def device(dy=None, dx=None, dz=None, other=False):
        along = y if dy is None else lax.rem(y + dy + NY, NY)
        across = x if dx is None else lax.rem(x + dx, NX)
        up = z if dz is None else lax.rem(z + dz, NZ)
        return {"grp": along * 2 + (1 - core if other else core), "graph": across * NZ + up}

    def remote(phase, slot, source, target, place):
        return pltpu.make_async_remote_copy(
            src_ref=source, dst_ref=target, send_sem=send_sem.at[phase, slot],
            recv_sem=recv_sem.at[phase, slot], device_id=place, device_id_type=MESH,
        )

    def each(count, body, first=1):
        def step(d, carry):
            body(d)
            return carry

        lax.fori_loop(first, count, step, 0)

    def lanes(k):
        return pl.ds(pl.multiple_of(k * 128, 128), 128)

    def arrived(phase, slot, ref):
        pltpu.make_async_copy(ref, ref, recv_sem.at[phase, slot]).wait()

    def left(phase, slot, ref):
        pltpu.make_async_copy(ref, ref, send_sem.at[phase, slot]).wait()

    loads = [
        pltpu.make_async_copy(source, target, load_sem.at[k])
        for k, (source, target) in enumerate((
            (w_hbm, w_own), (at_hbm, at_in), (co_hbm, co_in), (owner_hbm, index_in.at[0]),
            (slot_hbm, index_in.at[1]), (tslot_hbm, index_in.at[2]), (turn_hbm, index_in.at[3]),
            (rt_hbm, rt_in)))
    ]
    for load in loads:
        load.start()

    barrier = pltpu.get_barrier_semaphore()

    def greet(place):
        pl.semaphore_signal(barrier, inc=1, device_id=place, device_id_type=MESH)

    greet(device(other=True))
    each(5 * NX, lambda k: pl.when(k != 2 * NX)(
        lambda: greet(device(dy=lax.div(k, NX) - 2, dx=lax.rem(k, NX)))), 0)
    each(NZ, lambda d: greet(device(dz=d)))

    loads[0].wait()
    pl.semaphore_wait(barrier, 1 + 4 + 5 * (NX - 1) + (NZ - 1))
    core_copy = remote(PH_CORE, 0, w_own, w_sib, device(other=True))
    core_copy.start()

    loads[1].wait()
    for b in range(9):
        at48[0, b * 4:b * 4 + 4, :] = at_in[b].astype(F32)
    at48[0, 36:48, :] = jnp.zeros((12, 512), F32)
    for xb in range(NX):
        own_rows = at48[0, :, xb * 128:(xb + 1) * 128].astype(BF16)
        atx[NX, xb] = own_rows
        atx[x, xb] = own_rows
    each(NX, lambda d: remote(PH_ATX, 0, atx.at[NX], atx.at[x], device(dx=d)).start())

    core_copy.wait_recv()

    def share(dy, expert):
        return coef[lax.rem(y + dy + NY, NY) * 2 + core, expert].astype(F32) * (1.0 / 1024.0)

    own_first, other_first = grp * 2, (y * 2 + 1 - core) * 2

    def partial_of(dy, xb):
        at = lanes(xb)
        total = None
        for ref, first in ((w_own, own_first), (w_sib, other_first)):
            for e in range(2):
                term = share(dy, first + e) * ref[e, :, :, at].astype(F32)
                total = term if total is None else total + term
        return total

    halves = (pl.ds(0, 2), pl.ds(2, 2))
    def fill_y(k):
        slot = lax.div(k, NX)
        dy = jnp.where(slot == 0, -4, jnp.where(slot == 1, 3, -3))
        ybuf[slot, lax.rem(k, NX)] = partial_of(dy, lax.rem(k, NX)).astype(BF16)

    each(3 * NX, fill_y, 0)
    for h in range(2):
        remote(PH_Y, 3 * h, ybuf.at[0, halves[h]], yrecv.at[0, halves[h]], device(dy=(-2, 2)[h])).start()
    for slot, hop in ((1, 1), (2, -1)):
        remote(PH_Y, slot, ybuf.at[slot], yrecv.at[slot], device(dy=hop)).start()

    def yx_send(k, source, target, phase):
        dy = k - 2

        def piece(d):
            to = lax.rem(x + d, NX)

            @pl.when((k != 2) | (d != 0))
            def _():
                remote(phase, k, source(k, to), target.at[k, x], device(dy=dy, dx=d)).start()

        each(NX, piece, 0)

    def near_block(k):
        def fill(xb):
            yxbuf[k, xb] = partial_of(k - 2, xb).astype(BF16)

        each(NX, fill, 0)
        yx_send(k, lambda slot, to: yxbuf.at[slot, to], yxrecv, PH_YX)

    each(4, near_block, 1)
    yxrecv[2, x] = yxbuf[2, x]

    for load in loads[2:]:
        load.wait()
    for b in range(9):
        co80[0, b * 4:b * 4 + 4, :] = co_in[b].astype(F32)
    co80[0, 36:48, :] = jnp.zeros((12, 512), F32)

    def place(owner, slot):
        return (owner & 7) * 16 + (owner >> 3) * 4 + slot

    row = lax.broadcasted_iota(I32, (16, 128), 0)
    codes = jnp.where(row == 0, place(index_in[0], index_in[1]), 0)
    codes = jnp.where(row == 1, place(graph, index_in[2]), codes)
    codes = jnp.where(row == 2, index_in[3], codes).astype(F32).astype(BF16)
    for xb in range(NX):
        cox[NX + xb, 0:48, :] = co80[0, :, xb * 128:(xb + 1) * 128].astype(BF16)
        cox[NX + xb, 48:64, :] = codes
    each(NX, lambda d: remote(
        PH_COX, 0, cox.at[NX + lax.rem(x + d, NX)], cox.at[x], device(dx=d)).start())
    cox[x] = cox[NX + x]

    row, column = grid_of(144, 192)
    block, within = split48(column)
    order[...] = one_hot(
        ((within >> 2) == (row >> 4)) & (((row >> 2) & 3) == block) & ((within & 3) == (row & 3)))

    arrived(PH_ATX, 0, atx.at[pl.ds(0, NX - 1)])
    for xb in range(NX):
        stacked = jnp.concatenate([atx[s, xb] for s in range(NX)], axis=0)
        a_ref[z, :, :, xb * 128:(xb + 1) * 128] = dot(order[...], stacked).astype(BF16).reshape(9, 16, 128)

    row, column = grid_of(16, 192)
    block, within = split48(column)
    gather16[...] = one_hot(row == block * 4 + (within & 3))
    row, column = grid_of(192, 16)
    block, within = split48(row)
    expand[...] = one_hot(column == block * 4 + (within & 3))
    row, column = grid_of(192, 256)
    block, within = split48(row)
    same[...] = jnp.where((within >> 2) == (column >> 4), 1.0, 0.0)

    def selections(t):
        row, column = grid_of(128, 256)
        spread[t] = one_hot(((row >> 4) == t) & ((row & 15) == (column & 15)))
        row, column = grid_of(256, 128)
        fold[t] = one_hot(((column >> 4) == t) & ((row & 15) == (column & 15)))
        row, column = grid_of(128, 128)
        same16 = (row & 15) == (column & 15)

        def pair(k):
            mark = jnp.where(k >= 3, k + 1, k)
            perm[k, :, lanes(t)] = one_hot(((row >> 4) == t) & ((column >> 4) == mark) & same16)
            unperm[t, :, lanes(k)] = one_hot(((column >> 4) == t) & ((row >> 4) == mark) & same16)

        each(6, pair, 0)

    each(NZ, selections, 0)

    def right_copy(s):
        slot = lax.rem(z - s + NZ, NZ)
        return remote(PH_ATR, s, a_ref.at[slot], a_ref.at[slot], device(dz=1))

    def left_copy(s):
        slot = lax.rem(z + s, NZ)
        return remote(PH_ATL, s, a_ref.at[slot], a_ref.at[slot], device(dz=NZ - 1))

    arrived(PH_COX, 0, cox.at[pl.ds(0, NX - 1)])
    stacked = jnp.concatenate([cox[s, 0:48] for s in range(NX)], axis=0)

    def pack_cotangent(t):
        wide = (dot(stacked, spread[t]) * same[...]).astype(BF16)
        packed = dot(gather16[...], wide).astype(BF16)
        cobuf[t, 0] = packed[:, 0:128]
        cobuf[t, 1] = packed[:, 128:256]
        for s in range(NX):
            cobuf[t, 2 + s] = cox[s, 48:64]

    each(NZ, pack_cotangent, 0)
    each(NZ, lambda d: remote(
        PH_COZ, 0, cobuf.at[lax.rem(z + d, NZ)], corecv.at[z], device(dz=d)).start())
    corecv[z] = cobuf[z]
    right_copy(0).start()
    left_copy(0).start()

    for h in range(2):
        arrived(PH_Y, 3 * h, yrecv.at[0, halves[h]])
    for slot in (1, 2):
        arrived(PH_Y, slot, yrecv.at[slot])

    def far_block(h):
        k = 4 * h

        def fill(xb):
            total = partial_of(k - 2, xb) + yrecv[2 - h, xb].astype(F32)
            through = jnp.where(lax.div(xb, 2) == h, 1.0, 0.0)
            yxbuf[k, xb] = (total + through * yrecv[0, xb].astype(F32)).astype(BF16)

        each(NX, fill, 0)
        yx_send(k, lambda slot, to: yxbuf.at[slot, to], yxrecv, PH_YX)

    each(2, far_block, 0)

    for i in range(9):
        opening, closing = SPANS[DEGREE[i]]
        first = ENTRY[i, opening]
        rt35[first:first + closing - opening, :] = rt_in[i, opening:closing, :]
    rt35[35:40, :] = jnp.zeros((5, 64), F32)
    table = rt35[...]
    high = table.astype(BF16)
    rot2[:, 0:64] = high
    rot2[:, 64:128] = (table - high.astype(F32)).astype(BF16)

    arrived(PH_COZ, 0, corecv.at[pl.ds(0, NZ - 1)])
    for half in range(2):
        tall = jnp.transpose(corecv[:, half].reshape(128, 128).astype(F32)).astype(BF16)
        rows = 128 if half == 0 else 16
        cs[half * 128:half * 128 + rows, :] = tall[0:rows]

    def turned(entries, values, opening, closing, i):
        total = entries[i, opening] * values(opening)
        for b in range(opening + 1, closing):
            total = total + entries[i, b] * values(b)
        return total

    def entries_of(t, at):
        return {key: turns[t, k:k + 1, at] for key, k in ENTRY.items()}

    def prepare(t):
        def places(q):
            at = lanes(q)
            row = lax.broadcasted_iota(I32, (128, 128), 0)
            codes = corecv[t, 2 + q].astype(F32)
            oh[t, :, at] = one_hot(row.astype(F32) == codes[0:1])
            oh[NZ, :, at] = one_hot(row.astype(F32) == codes[1:2])
            oh[NZ + 1, :, at] = one_hot((row & 63).astype(F32) == codes[2:3])

        def messages(q):
            at = lanes(q)
            entries = entries_of(t, at)
            for opening, closing in SPANS:
                for i in range(opening, closing):
                    grads_at[t, i * 16:(i + 1) * 16, at] = turned(
                        entries, lambda b: ch[b * 16:(b + 1) * 16, at], opening, closing, i)

        each(NX, places, 0)
        ch[...] = dot(cs[...], oh[NZ])
        turns[t] = dot(rot2[...], oh[NZ + 1])
        each(NX, messages, 0)

    def pass_on(right, left_way, s):
        right(s - 1).wait_recv()
        right(s).start()
        left_way(s - 1).wait_recv()

        @pl.when(s < 3)
        def _():
            left_way(s).start()

    def prepare_and_pass(t):
        @pl.when((lax.rem(t, 2) == 0) & (t < 6))
        def _():
            pass_on(right_copy, left_copy, lax.div(t, 2) + 1)

        prepare(t)

    each(4, prepare_and_pass, 0)

    for k, dy in enumerate(NEAR):
        arrived(PH_YX, k, yxrecv.at[k] if dy else yxrecv.at[k, pl.ds(0, NX - 1)])

    def mix(k):
        s, l = lax.div(k, 3), lax.rem(k, 3)
        total = yxrecv[0, s, l].astype(F32)
        for near in range(1, 5):
            total = total + yxrecv[near, s, l].astype(F32)
        mx[s, l] = total.astype(BF16)

    each(3 * NX, mix, 0)

    def pack_maps(k, total):
        h, l = lax.div(k, 3), lax.rem(k, 3)
        return total + dot(mx[pl.ds(2 * h, 2), l].reshape(32, 128), perm[k])

    packed = lax.fori_loop(0, 6, pack_maps, jnp.zeros((32, 1024), F32))
    packed = packed.astype(BF16)
    for t in range(NZ):
        mzbuf[t] = packed[:, t * 128:(t + 1) * 128].reshape(2, 16, 128)
    each(NZ, lambda d: remote(
        PH_MZ, 0, mzbuf.at[lax.rem(z + d, NZ)], wc.at[z], device(dz=d)).start())
    wc[z] = mzbuf[z]
    mc[z] = mx[...]
    each(8, prepare_and_pass, 4)
    right_copy(3).wait_recv()
    arrived(PH_MZ, 0, wc.at[pl.ds(0, NZ - 1)])

    def maps_right(s):
        slot = lax.rem(z - s + NZ, NZ)
        return remote(PH_MC, s, mc.at[slot], mc.at[slot], device(dz=1))

    def maps_left(s):
        slot = lax.rem(z + s, NZ)
        return remote(PH_MCL, s, mc.at[slot], mc.at[slot], device(dz=NZ - 1))

    maps_right(0).start()
    maps_left(0).start()

    columns16 = jnp.concatenate(
        [jnp.concatenate([wc[t, s] for t in range(NZ)], axis=0) for s in range(2)], axis=0)
    flipped = jnp.transpose(columns16.astype(F32)).astype(BF16)
    for l in range(3):
        for h in range(2):
            first = h * 64 + l * 16
            maps16[l, :, h * 256:(h + 1) * 256] = flipped[first:first + 16]

    def degree_of(b):
        return jnp.where(b >= 1, 1, 0) + jnp.where(b >= 4, 1, 0)

    def rows16(b):
        return pl.ds(pl.multiple_of(b * 16, 16), 16)

    def atom_maps(b):
        hs[rows16(b), :] = dot(maps16[degree_of(b)], a_ref[:, b].reshape(128, 512), NT).astype(BF16)

    each(9, atom_maps, 0)

    g_acc[...] = jnp.zeros(g_acc.shape, F32)

    def edges(t):
        hh[...] = dot(hs[...], oh[t])

        def group(q):
            at = lanes(q)
            entries = entries_of(t, at)
            grads, inner, gate = [], None, None
            for opening, closing in SPANS:
                for i in range(opening, closing):
                    hidden = turned(entries, lambda b: hh[b * 16:(b + 1) * 16, at], opening, closing, i)
                    grad = grads_at[t, i * 16:(i + 1) * 16, at]
                    if i == 0:
                        gate = jax.nn.sigmoid(hidden)
                    inner = grad * hidden if inner is None else inner + grad * hidden
                    grads.append(grad * gate)
            grads[0] = grads[0] + inner * gate * (1.0 - gate)
            for opening, closing in SPANS:
                for b in range(opening, closing):
                    total = entries[opening, b] * grads[opening]
                    for i in range(opening + 1, closing):
                        total = total + entries[i, b] * grads[i]
                    u_ref[b * 16:(b + 1) * 16, at] = total.astype(BF16)

        each(NX, group, 0)
        g_acc[...] += dot(u_ref[...], oh[t], NT)

        @pl.when((lax.rem(t, 2) == 1) & (t < 6))
        def _():
            pass_on(maps_right, maps_left, lax.div(t + 1, 2))

    each(NZ, edges, 0)

    sums = g_acc[...]
    narrow[...] = sums.astype(BF16)
    for h in range(2):
        sgt[h * 64 + 48:h * 64 + 64, :] = jnp.zeros((16, 256), F32)
    for l, (opening, closing) in enumerate(SPANS):
        total = lax.fori_loop(
            opening, closing,
            lambda b, total: total + dot(narrow[rows16(b), :], a_ref[:, b].reshape(128, 512)),
            jnp.zeros((16, 512), F32))
        for h in range(2):
            sgt[h * 64 + l * 16:h * 64 + (l + 1) * 16, :] = total[:, h * 256:(h + 1) * 256]
    tall = jnp.transpose(sgt[...]).astype(BF16)
    for t in range(NZ):
        for s in range(2):
            first = s * 128 + t * 16
            sgbuf[t, s] = tall[first:first + 16]
    each(NZ, lambda d: remote(
        PH_SZ, 0, sgbuf.at[lax.rem(z + d, NZ)], sgrecv.at[z], device(dz=d)).start())
    sgrecv[z] = sgbuf[z]
    turned_sums = jnp.transpose(
        jnp.concatenate([sums, jnp.zeros((112, 128), F32)], axis=0)).astype(BF16)
    for t in range(NZ):
        gbuf[t] = turned_sums[t * 16:(t + 1) * 16]
    each(NZ, lambda d: remote(
        PH_GZ, 0, gbuf.at[lax.rem(z + d, NZ)], grecv.at[z], device(dz=d)).start())
    grecv[z] = gbuf[z]

    arrived(PH_SZ, 0, sgrecv.at[pl.ds(0, NZ - 1)])
    rows = lax.fori_loop(
        0, NZ, lambda t, total: total + dot(sgrecv[t].reshape(32, 128), unperm[t]),
        jnp.zeros((32, 768), F32))
    for s in range(NX):
        for l in range(3):
            at = (s // 2 * 3 + l) * 128
            sg4[s, l] = rows[s % 2 * 16:s % 2 * 16 + 16, at:at + 128].astype(BF16)

    each(5, lambda k: yx_send(k, lambda slot, to: sg4.at[to], sgx, PH_SYX), 0)
    sgx[2, x] = sg4[x]

    arrived(PH_GZ, 0, grecv.at[pl.ds(0, NZ - 1)])

    def unpack(t, total):
        wide = (dot(expand[...], grecv[t]) * same[...]).astype(BF16)
        return total + dot(wide, fold[t])

    held = lax.fori_loop(0, NZ, unpack, jnp.zeros((192, 128), F32))

    arrived(PH_SYX, 0, sgx.at[0])
    arrived(PH_SYX, 4, sgx.at[4])
    for h, k, hop in ((0, 0, -2), (1, 4, 2)):
        remote(PH_FW, 3 * h, sgx.at[k, halves[h]], forwarded.at[0, halves[h]], device(dy=hop)).start()
    for slot, k, hop in ((1, 4, 1), (2, 0, -1)):
        remote(PH_FW, slot, sgx.at[k], forwarded.at[slot], device(dy=hop)).start()

    maps_right(3).wait_recv()
    coefficient = split48(lax.broadcasted_iota(I32, (192, 128), 0))[1] >> 2
    parts = jnp.zeros((192, 512), F32)
    for l, (opening, closing) in enumerate(SPANS):
        inside = (coefficient >= opening) & (coefficient < closing)
        maps = jnp.concatenate(
            [jnp.concatenate([mc[t, s, l] for t in range(NZ)], axis=0) for s in range(NX)], axis=0)
        parts = parts + dot(jnp.where(inside, held, 0.0).astype(BF16), maps, NT)
    for s in range(NX):
        gxbuf[s] = parts[s * 48:(s + 1) * 48].astype(BF16)
    each(NX, lambda d: remote(
        PH_GX, 0, gxbuf.at[lax.rem(x + d, NX)], gxrecv.at[d], device(dx=d)).start())
    gxrecv[0] = gxbuf[x]
    for k in (1, 2, 3):
        arrived(PH_SYX, k, sgx.at[k] if NEAR[k] else sgx.at[k, pl.ds(0, NX - 1)])
    arrived(PH_GX, 0, gxrecv.at[pl.ds(0, NX - 1)])
    total = gxrecv[0].astype(F32)
    for s in range(1, NX):
        total = total + gxrecv[s].astype(F32)
    for b in range(9):
        ga_ref[b] = total[b * 4:b * 4 + 4]

    for h in range(2):
        arrived(PH_FW, 3 * h, forwarded.at[0, halves[h]])
    for slot in (1, 2):
        arrived(PH_FW, slot, forwarded.at[slot])

    def expert_sum(expert, s):
        total = None
        for k, dy in enumerate(NEAR):
            term = share(-dy, expert) * sgx[k, s].astype(F32)
            total = term if total is None else total + term
        for slot, dy in ((0, 4), (1, -3), (2, 3)):
            total = total + share(dy, expert) * forwarded[slot, s].astype(F32)
        return total

    def other_half(k):
        e, s = lax.div(k, NX), lax.rem(k, NX)
        endbuf[e, s] = expert_sum(other_first + e, s).astype(BF16)

    def own_half(k):
        e, s = lax.div(k, NX), lax.rem(k, NX)
        ge_ref[e, :, :, lanes(s)] = expert_sum(own_first + e, s)

    def both_halves(k):
        e, s = lax.div(k, NX), lax.rem(k, NX)
        ge_ref[e, :, :, lanes(s)] += endrecv[e, s].astype(F32)

    each(2 * NX, other_half, 0)
    end_copy = remote(PH_END, 0, endbuf, endrecv, device(other=True))
    end_copy.start()
    each(2 * NX, own_half, 0)
    end_copy.wait_recv()
    each(2 * NX, both_halves, 0)

    core_copy.wait_send()
    end_copy.wait_send()
    for s in range(4):
        right_copy(s).wait_send()
        maps_right(s).wait_send()
    for s in range(3):
        left_copy(s).wait_send()
        maps_left(s).wait_send()
    for phase, ref in ((PH_Y, ybuf), (PH_FW, forwarded)):
        for h in range(2):
            left(phase, 3 * h, ref.at[0, halves[h]])
        for slot in (1, 2):
            left(phase, slot, ref.at[slot])
    for k, dy in enumerate(NEAR):
        left(PH_YX, k, yxbuf.at[k] if dy else yxbuf.at[k, pl.ds(0, NX - 1)])
        left(PH_SYX, k, sg4 if dy else sg4.at[pl.ds(0, NX - 1)])
    left(PH_ATX, 0, atx.at[pl.ds(0, NX - 1)])
    left(PH_COX, 0, cox.at[pl.ds(0, NX - 1)])
    left(PH_GX, 0, gxbuf.at[pl.ds(0, NX - 1)])
    left(PH_COZ, 0, cobuf.at[pl.ds(0, NZ - 1)])
    left(PH_MZ, 0, mzbuf.at[pl.ds(0, NZ - 1)])
    left(PH_SZ, 0, sgbuf.at[pl.ds(0, NZ - 1)])
    left(PH_GZ, 0, gbuf.at[pl.ds(0, NZ - 1)])


def shards(
    atoms, cotangent, expert_weights, coefficients, src_owner, src_slot, tgt_slot, rot_index, rot_table
):
    hbm = pl.BlockSpec(memory_space=pltpu.HBM)
    vmem = pl.BlockSpec(memory_space=pltpu.VMEM)
    smem = pl.BlockSpec(memory_space=pltpu.SMEM)

    def b16(*shape):
        return pltpu.VMEM(shape, BF16)

    def f32(*shape):
        return pltpu.VMEM(shape, F32)

    grad_atoms, grad_experts = pl.pallas_call(
        kernel,
        out_shape=(
            jax.ShapeDtypeStruct((9, 4, 512), F32),
            jax.ShapeDtypeStruct((2, 3, 16, 512), F32),
        ),
        in_specs=[smem] + [hbm] * 8,
        out_specs=(vmem, vmem),
        scratch_shapes=[
            b16(2, 3, 16, 512),
            b16(2, 3, 16, 512),
            b16(9, 4, 512),
            b16(9, 4, 512),
            pltpu.VMEM((4, 1, 128), I32),
            f32(9, 9, 64),
            f32(40, 64),
            b16(3, NX, 3, 16, 128),
            b16(3, NX, 3, 16, 128),
            b16(5, NX, 3, 16, 128),
            b16(5, NX, 3, 16, 128),
            b16(NX, 3, 16, 128),
            b16(NZ, 2, 16, 128),
            b16(NZ, 2, 16, 128),
            b16(NZ, NX, 3, 16, 128),
            b16(3, 16, 512),
            f32(1, 48, 512),
            b16(NX + 1, NX, 48, 128),
            b16(NZ, 9, 16, 512),
            f32(1, 48, 512),
            b16(2 * NX, 64, 128),
            b16(NZ, 6, 16, 128),
            b16(NZ, 6, 16, 128),
            b16(192, 16),
            b16(NZ, 256, 128),
            b16(NZ, 128, 256),
            b16(6, 128, 1024),
            b16(NZ, 128, 768),
            b16(144, 192),
            b16(16, 192),
            f32(192, 256),
            b16(40, 128),
            b16(144, 128),
            b16(144, 128),
            f32(144, 512),
            f32(144, 512),
            f32(NZ, 144, 512),
            f32(NZ, 40, 512),
            b16(NZ + 2, 128, 512),
            b16(144, 512),
            f32(144, 128),
            b16(144, 128),
            b16(NZ, 16, 256),
            b16(NZ, 16, 256),
            b16(NX, 48, 512),
            b16(NX, 48, 512),
            f32(128, 256),
            b16(NZ, 2, 16, 128),
            b16(NZ, 2, 16, 128),
            b16(NX, 3, 16, 128),
            b16(5, NX, 3, 16, 128),
            b16(3, NX, 3, 16, 128),
            b16(2, NX, 3, 16, 128),
            b16(2, NX, 3, 16, 128),
            pltpu.SemaphoreType.DMA((8,)),
            pltpu.SemaphoreType.DMA((17, 5)),
            pltpu.SemaphoreType.DMA((17, 5)),
        ],
        compiler_params=pltpu.CompilerParams(
            collective_id=0, has_side_effects=True, vmem_limit_bytes=60 * 1024 * 1024
        ),
        cost_estimate=pl.CostEstimate(
            flops=2_000_000_000, bytes_accessed=1_000_000, transcendentals=65536
        ),
    )(
        coefficients, expert_weights, atoms[0].transpose(1, 0, 2), cotangent[0].transpose(1, 0, 2),
        src_owner.reshape(1, -1), src_slot, tgt_slot, rot_index, rot_table.transpose(1, 2, 0),
    )
    return grad_atoms.transpose(1, 0, 2)[None], grad_experts


def solution(mesh):
    placed = (
        P("grp", "graph", None, None),
        P("grp", "graph", None, None),
        P("grp", None, "graph", None),
        P(),
        P("grp", "graph", None),
        P("grp", "graph"),
        P("grp", "graph"),
        P("grp", "graph"),
        P(),
    )
    return jax.shard_map(
        shards,
        mesh=mesh,
        in_specs=placed,
        out_specs=(P("grp", "graph", None, None), P("grp", None, "graph", None)),
        check_vma=False,
    )
```

time: 79 us -> 89.2 us (1.13)
  Pallas kernels: 75 us -> 85.2 us
    pallas_call x1, Pallas kernels: 75 us -> 85.2 us  [shards(): pl.pallas_call(kernel, out_shape=(jax.ShapeDtypeStruct((9, 4, 512), F32),...]
where the time goes in v2:
time: 89.2 us; the launch traced here: 89 us
  Pallas kernels  85.2 us (96%)
  local copies, waits for them, and re-layouts  3.14 us (4%)
    pallas_call x1, Pallas kernels, shards(): pl.pallas_call(kernel, out_shape=(jax.ShapeDtypeStruct((9, 4, 512), F32),...  85.2 us
    unnamed x2, local copies, waits for them, and re-layouts  3.14 us

profile of v2, /device:TPU:1, one launch (start us, length us, event | category | flops | bytes accessed | tf_op | source)
XLA Modules:
  0.0 89.0 jit_solution(12258005686473203558)
XLA Ops:
  0.6 85.2 %shard_map.104 = (f32[9,4,512]{2,1,0:T(4,128)}, f32[2,3,16,512]{3,2,1,0:T(8,128)}) custom-call(s32[16,32]{1,0:T(8,128)} %coef.1, bf16[2,3,16,512]{3,2,1,0:T(8,128)(2,1)} %w_hbm.1, bf16[9,4,512]{2,1,0:T(4,128)(2,1)} %bitcast.13, bf16[9,4,512]{2,1,0:T(4,128)(2,1)} %bitcast.14, s32[1,128]{1,0:T(1,128)} %bitcast.15, s32[1,128]{1,0:T(1,128)} %slot_hbm.1, ...), custom_call_target="tpu_custom_call" | custom-call | flops 2000000000 | bytes 1000000 | tf_op jit(solution)/shard_map/pallas_call | solution.py:577
  85.8 1.5 %copy.13 = f32[1,4,9,512]{3,1,2,0:T(4,128)} copy(f32[1,4,9,512]{3,1,2,0:T(4,128)} %bitcast.11) | data formatting | bytes 147456
  87.4 1.6 %copy.14 = f32[2,3,16,512]{3,2,1,0:T(8,128)} copy(f32[2,3,16,512]{3,2,1,0:T(8,128)} %get-tuple-element.9) | data formatting | bytes 393216

commit v3 on v1

--- a/solution.py
+++ b/solution.py
@@ -14,7 +14,7 @@
 NT = (((1,), (1,)), ((), ()))
 
 (PH_CORE, PH_Y, PH_YX, PH_ATX, PH_ATR, PH_ATL, PH_COX, PH_COZ, PH_MZ, PH_MC,
- PH_GZ, PH_GX, PH_SZ, PH_SYX, PH_FW, PH_END) = range(16)
+ PH_GZ, PH_GX, PH_SZ, PH_SYX, PH_FW, PH_END, PH_MCL) = range(17)
 NEAR = (-2, -1, 0, 1, 2)
 ENTRY = {}
 for _opening, _closing in SPANS:
@@ -121,12 +121,14 @@
         spread[t] = one_hot(((row >> 4) == t) & ((row & 15) == (column & 15)))
         row, column = grid_of(256, 128)
         fold[t] = one_hot(((column >> 4) == t) & ((row & 15) == (column & 15)))
-        for l in range(3):
-            row, column = grid_of(128, 128)
-            perm[l, :, t * 128:(t + 1) * 128] = one_hot(
-                ((row >> 4) == t) & ((column >> 4) == l) & ((row & 15) == (column & 15)))
-            unperm[t, :, l * 128:(l + 1) * 128] = one_hot(
-                ((column >> 4) == t) & ((row >> 4) == l) & ((row & 15) == (column & 15)))
+        row, column = grid_of(128, 128)
+        same16 = (row & 15) == (column & 15)
+        for h in range(2):
+            for l in range(3):
+                perm[l, h, :, t * 128:(t + 1) * 128] = one_hot(
+                    ((row >> 4) == t) & ((column >> 4) == h * 4 + l) & same16)
+                unperm[t, :, (h * 3 + l) * 128:(h * 3 + l + 1) * 128] = one_hot(
+                    ((column >> 4) == t) & ((row >> 4) == h * 4 + l) & same16)
 
     for load in loads:
         load.wait()
@@ -178,8 +180,14 @@
                 total = term if total is None else total + term
         return total
 
-    steps = ((0, -4, -2), (1, 3, 1), (2, -3, -1))
-    for slot, dy, hop in steps:
+    halves = (pl.ds(0, 2), pl.ds(2, 2))
+    for xb in range(NX):
+        ybuf[0, xb] = partial_of(-4, xb).astype(BF16)
+        if xb % 2:
+            h = xb // 2
+            remote(PH_Y, 3 * h, ybuf.at[0, halves[h]], yrecv.at[0, halves[h]],
+                   device(dy=(-2, 2)[h])).start()
+    for slot, dy, hop in ((1, 3, 1), (2, -3, -1)):
         for xb in range(NX):
             ybuf[slot, xb] = partial_of(dy, xb).astype(BF16)
         remote(PH_Y, slot, ybuf.at[slot], yrecv.at[slot], device(dy=hop)).start()
@@ -226,14 +234,17 @@
     right_copy(0).start()
     left_copy(0).start()
 
-    for slot in range(3):
+    for h in range(2):
+        arrived(PH_Y, 3 * h, yrecv.at[0, halves[h]])
+    for slot in (1, 2):
         arrived(PH_Y, slot, yrecv.at[slot])
-    for xb in range(NX):
-        yxbuf[0, xb] = (partial_of(-2, xb) + yrecv[0, xb].astype(F32) + yrecv[2, xb].astype(F32)).astype(BF16)
-    yx_send(0)
-    for xb in range(NX):
-        yxbuf[4, xb] = (partial_of(2, xb) + yrecv[1, xb].astype(F32)).astype(BF16)
-    yx_send(4)
+    for k, dy, slot in ((0, -2, 2), (4, 2, 1)):
+        for xb in range(NX):
+            total = partial_of(dy, xb) + yrecv[slot, xb].astype(F32)
+            if (xb >= 2) == (k == 4):
+                total = total + yrecv[0, xb].astype(F32)
+            yxbuf[k, xb] = total.astype(BF16)
+        yx_send(k)
 
     for i in range(9):
         opening, closing = SPANS[DEGREE[i]]
@@ -294,17 +305,18 @@
 
     for k, dy in enumerate(NEAR):
         arrived(PH_YX, k, yxrecv.at[k] if dy else yxrecv.at[k, pl.ds(0, NX - 1)])
-    packed = jnp.zeros((64, 1024), F32)
+    packed = jnp.zeros((32, 1024), F32)
     for l in range(3):
         for s in range(NX):
             total = yxrecv[0, s, l].astype(F32)
             for k in range(1, 5):
                 total = total + yxrecv[k, s, l].astype(F32)
             mx[s, l] = total.astype(BF16)
-        packed = packed + dot(mx[:, l].reshape(64, 128), perm[l])
+        for h in range(2):
+            packed = packed + dot(mx[2 * h:2 * h + 2, l].reshape(32, 128), perm[l, h])
     packed = packed.astype(BF16)
     for t in range(NZ):
-        mzbuf[t] = packed[:, t * 128:(t + 1) * 128].reshape(NX, 16, 128)
+        mzbuf[t] = packed[:, t * 128:(t + 1) * 128].reshape(2, 16, 128)
     each(NZ, lambda d: remote(
         PH_MZ, 0, mzbuf.at[lax.rem(z + d, NZ)], wc.at[z], device(dz=d)).start())
     wc[z] = mzbuf[z]
@@ -316,24 +328,23 @@
     each(NZ, lambda d: remote(PH_MC, 0, mx, mc.at[z], device(dz=d)).start())
 
     columns16 = jnp.concatenate(
-        [jnp.concatenate([wc[t, s] for t in range(NZ)], axis=0) for s in range(NX)], axis=0)
+        [jnp.concatenate([wc[t, s] for t in range(NZ)], axis=0) for s in range(2)], axis=0)
     flipped = jnp.transpose(columns16.astype(F32)).astype(BF16)
     for b in range(9):
         l = DEGREE[b]
-        hs[b * 16:(b + 1) * 16, :] = dot(
-            flipped[l * 16:(l + 1) * 16], a_ref[:, b].reshape(128, 512), NT).astype(BF16)
-
-    g_acc[...] = jnp.zeros(g_acc.shape, F32)
-
-    def edges(t, carry):
-        hh[...] = dot(hs[...], oh[t])
+        maps = jnp.concatenate([flipped[h * 64 + l * 16:h * 64 + (l + 1) * 16] for h in range(2)], axis=1)
+        hs[b * 16:(b + 1) * 16, :] = dot(maps, a_ref[:, b].reshape(128, 512), NT).astype(BF16)
+
+
+    def edges(t):
+        hh[t] = dot(hs[...], oh[t])
         for q in range(NX):
             at = slice(q * 128, (q + 1) * 128)
             entries = entries_of(t, at)
             grads, inner, gate = [], None, None
             for opening, closing in SPANS:
                 for i in range(opening, closing):
-                    hidden = turned(entries, lambda b: hh[b * 16:(b + 1) * 16, at], opening, closing, i)
+                    hidden = turned(entries, lambda b: hh[t, b * 16:(b + 1) * 16, at], opening, closing, i)
                     grad = grads_at[t, i * 16:(i + 1) * 16, at]
                     if i == 0:
                         gate = jax.nn.sigmoid(hidden)
@@ -345,23 +356,26 @@
                     total = entries[opening, b] * grads[opening]
                     for i in range(opening + 1, closing):
                         total = total + entries[i, b] * grads[i]
-                    u_ref[b * 16:(b + 1) * 16, at] = total.astype(BF16)
-        g_acc[...] += dot(u_ref[...], oh[t], NT)
-        return carry
-
-    lax.fori_loop(0, NZ, edges, 0)
+                    u_ref[t, b * 16:(b + 1) * 16, at] = total.astype(BF16)
+
+    for t in range(NZ):
+        edges(t)
+    wide_u = jnp.concatenate([u_ref[t] for t in range(NZ)], axis=1)
+    g_acc[...] = dot(wide_u, jnp.concatenate([oh[t] for t in range(NZ)], axis=1), NT)
 
     sums = g_acc[...]
     narrow = sums.astype(BF16)
-    sgt[48:128, :] = jnp.zeros((80, 512), F32)
+    for h in range(2):
+        sgt[h * 64 + 48:h * 64 + 64, :] = jnp.zeros((16, 256), F32)
     for l, (opening, closing) in enumerate(SPANS):
         total = jnp.zeros((16, 512), F32)
         for b in range(opening, closing):
             total = total + dot(narrow[b * 16:(b + 1) * 16], a_ref[:, b].reshape(128, 512))
-        sgt[l * 16:(l + 1) * 16, :] = total
+        for h in range(2):
+            sgt[h * 64 + l * 16:h * 64 + (l + 1) * 16, :] = total[:, h * 256:(h + 1) * 256]
     tall = jnp.transpose(sgt[...]).astype(BF16)
     for t in range(NZ):
-        for s in range(NX):
+        for s in range(2):
             first = s * 128 + t * 16
             sgbuf[t, s] = tall[first:first + 16]
     each(NZ, lambda d: remote(
@@ -376,12 +390,13 @@
     grecv[z] = gbuf[z]
 
     arrived(PH_SZ, 0, sgrecv.at[pl.ds(0, NZ - 1)])
-    rows = dot(sgrecv[0].reshape(64, 128), unperm[0])
+    rows = dot(sgrecv[0].reshape(32, 128), unperm[0])
     for t in range(1, NZ):
-        rows = rows + dot(sgrecv[t].reshape(64, 128), unperm[t])
+        rows = rows + dot(sgrecv[t].reshape(32, 128), unperm[t])
     for s in range(NX):
         for l in range(3):
-            sg4[s, l] = rows[s * 16:(s + 1) * 16, l * 128:(l + 1) * 128].astype(BF16)
+            at = (s // 2 * 3 + l) * 128
+            sg4[s, l] = rows[s % 2 * 16:s % 2 * 16 + 16, at:at + 128].astype(BF16)
 
     for k in (0, 4, 1, 3, 2):
         dy = NEAR[k]
@@ -400,8 +415,9 @@
 
     arrived(PH_SYX, 0, sgx.at[0])
     arrived(PH_SYX, 4, sgx.at[4])
-    onward = ((0, 0, -2), (1, 4, 1), (2, 0, -1))
-    for slot, k, hop in onward:
+    for h, k, hop in ((0, 0, -2), (1, 4, 2)):
+        remote(PH_FW, 3 * h, sgx.at[k, halves[h]], forwarded.at[0, halves[h]], device(dy=hop)).start()
+    for slot, k, hop in ((1, 4, 1), (2, 0, -1)):
         remote(PH_FW, slot, sgx.at[k], forwarded.at[slot], device(dy=hop)).start()
 
     arrived(PH_MC, 0, mc.at[pl.ds(0, NZ - 1)])
@@ -426,7 +442,9 @@
     for b in range(9):
         ga_ref[b] = total[b * 4:b * 4 + 4]
 
-    for slot in range(3):
+    for h in range(2):
+        arrived(PH_FW, 3 * h, forwarded.at[0, halves[h]])
+    for slot in (1, 2):
         arrived(PH_FW, slot, forwarded.at[slot])
 
     def expert_sum(expert, s):
@@ -457,9 +475,11 @@
         right_copy(s).wait_send()
     for s in range(3):
         left_copy(s).wait_send()
-    for slot in range(3):
-        left(PH_Y, slot, ybuf.at[slot])
-        left(PH_FW, slot, forwarded.at[slot])
+    for phase, ref in ((PH_Y, ybuf), (PH_FW, forwarded)):
+        for h in range(2):
+            left(phase, 3 * h, ref.at[0, halves[h]])
+        for slot in (1, 2):
+            left(phase, slot, ref.at[slot])
     for k, dy in enumerate(NEAR):
         left(PH_YX, k, yxbuf.at[k] if dy else yxbuf.at[k, pl.ds(0, NX - 1)])
         left(PH_SYX, k, sg4 if dy else sg4.at[pl.ds(0, NX - 1)])
@@ -507,8 +527,8 @@
             b16(5, NX, 3, 16, 128),
             b16(5, NX, 3, 16, 128),
             b16(NX, 3, 16, 128),
-            b16(NZ, NX, 16, 128),
-            b16(NZ, NX, 16, 128),
+            b16(NZ, 2, 16, 128),
+            b16(NZ, 2, 16, 128),
             b16(NZ, NX, 3, 16, 128),
             f32(1, 48, 512),
             b16(NX + 1, NX, 48, 128),
@@ -520,36 +540,36 @@
             b16(192, 16),
             b16(NZ, 256, 128),
             b16(NZ, 128, 256),
-            b16(3, 128, 1024),
-            b16(NZ, 128, 384),
+            b16(3, 2, 128, 1024),
+            b16(NZ, 128, 768),
             b16(144, 192),
             b16(16, 192),
             f32(192, 256),
             b16(40, 128),
             b16(144, 128),
             b16(144, 128),
-            f32(144, 512),
+            f32(NZ, 144, 512),
             f32(144, 512),
             f32(NZ, 144, 512),
             f32(NZ, 40, 512),
             b16(NZ + 2, 128, 512),
-            b16(144, 512),
+            b16(NZ, 144, 512),
             f32(144, 128),
             b16(NZ, 16, 256),
             b16(NZ, 16, 256),
             b16(NX, 48, 512),
             b16(NX, 48, 512),
-            f32(128, 512),
-            b16(NZ, NX, 16, 128),
-            b16(NZ, NX, 16, 128),
+            f32(128, 256),
+            b16(NZ, 2, 16, 128),
+            b16(NZ, 2, 16, 128),
             b16(NX, 3, 16, 128),
             b16(5, NX, 3, 16, 128),
             b16(3, NX, 3, 16, 128),
             b16(2, NX, 3, 16, 128),
             b16(2, NX, 3, 16, 128),
             pltpu.SemaphoreType.DMA((8,)),
-            pltpu.SemaphoreType.DMA((16, 5)),
-            pltpu.SemaphoreType.DMA((16, 5)),
+            pltpu.SemaphoreType.DMA((17, 5)),
+            pltpu.SemaphoreType.DMA((17, 5)),
         ],
         compiler_params=pltpu.CompilerParams(
             collective_id=0, has_side_effects=True, vmem_limit_bytes=60 * 1024 * 1024

time: 79 us -> 77.2 us (0.977)
  Pallas kernels: 75 us -> 73.2 us
    pallas_call x1, Pallas kernels: 75 us -> 73.2 us  [shards(): pl.pallas_call(kernel, out_shape=(jax.ShapeDtypeStruct((9, 4, 512), F32),...]
where the time goes in v3:
time: 77.2 us; the launch traced here: 76.9 us
  Pallas kernels  73.2 us (95%)
  local copies, waits for them, and re-layouts  3.14 us (4%)
    pallas_call x1, Pallas kernels, shards(): pl.pallas_call(kernel, out_shape=(jax.ShapeDtypeStruct((9, 4, 512), F32),...  73.2 us
    unnamed x2, local copies, waits for them, and re-layouts  3.14 us

profile of v3, /device:TPU:1, one launch (start us, length us, event | category | flops | bytes accessed | tf_op | source)
XLA Modules:
  0.0 76.9 jit_solution(4521246665762400453)
XLA Ops:
  0.6 73.2 %shard_map.104 = (f32[9,4,512]{2,1,0:T(4,128)}, f32[2,3,16,512]{3,2,1,0:T(8,128)}) custom-call(s32[16,32]{1,0:T(8,128)} %coef.1, bf16[2,3,16,512]{3,2,1,0:T(8,128)(2,1)} %w_hbm.1, bf16[9,4,512]{2,1,0:T(4,128)(2,1)} %bitcast.13, bf16[9,4,512]{2,1,0:T(4,128)(2,1)} %bitcast.14, s32[1,128]{1,0:T(1,128)} %bitcast.15, s32[1,128]{1,0:T(1,128)} %slot_hbm.1, ...), custom_call_target="tpu_custom_call" | custom-call | flops 2000000000 | bytes 1000000 | tf_op jit(solution)/shard_map/pallas_call | solution.py:509
  73.8 1.5 %copy.13 = f32[1,4,9,512]{3,1,2,0:T(4,128)} copy(f32[1,4,9,512]{3,1,2,0:T(4,128)} %bitcast.11) | data formatting | bytes 147456
  75.3 1.6 %copy.14 = f32[2,3,16,512]{3,2,1,0:T(8,128)} copy(f32[2,3,16,512]{3,2,1,0:T(8,128)} %get-tuple-element.9) | data formatting | bytes 393216

commit v4 on v3

--- a/solution.py
+++ b/solution.py
@@ -36,6 +36,11 @@
     return lax.broadcasted_iota(I32, shape, 0), lax.broadcasted_iota(I32, shape, 1)
 
 
+def roll16(block, by):
+    by = by * 16 % 128
+    return pltpu.roll(block, by, 1) if by else block
+
+
 def split48(index):
     block = jnp.where(index >= 48, 1, 0) + jnp.where(index >= 96, 1, 0) + jnp.where(index >= 144, 1, 0)
     return block, index - 48 * block
@@ -47,7 +52,7 @@
     w_own, w_sib, at_in, co_in, index_in, rt_in, rt35,
     ybuf, yrecv, yxbuf, yxrecv, mx, mzbuf, wc, mc,
     at48, atx, a_ref, co80, cox, cobuf, corecv,
-    expand, fold, spread, perm, unperm, order, gather16, same, rot2,
+    expand, fold, spread, order, gather16, same, rot2,
     hs, cs, hh, ch, grads_at, turns, oh, u_ref, g_acc, gbuf, grecv, gxbuf, gxrecv,
     sgt, sgbuf, sgrecv, sg4, sgx, forwarded, endbuf, endrecv,
     load_sem, send_sem, recv_sem,
@@ -110,25 +115,12 @@
     row, column = grid_of(16, 192)
     block, within = split48(column)
     gather16[...] = one_hot(row == block * 4 + (within & 3))
-    row, column = grid_of(192, 16)
-    block, within = split48(row)
-    expand[...] = one_hot(column == block * 4 + (within & 3))
     row, column = grid_of(192, 256)
     block, within = split48(row)
     same[...] = jnp.where((within >> 2) == (column >> 4), 1.0, 0.0)
     for t in range(NZ):
         row, column = grid_of(128, 256)
         spread[t] = one_hot(((row >> 4) == t) & ((row & 15) == (column & 15)))
-        row, column = grid_of(256, 128)
-        fold[t] = one_hot(((column >> 4) == t) & ((row & 15) == (column & 15)))
-        row, column = grid_of(128, 128)
-        same16 = (row & 15) == (column & 15)
-        for h in range(2):
-            for l in range(3):
-                perm[l, h, :, t * 128:(t + 1) * 128] = one_hot(
-                    ((row >> 4) == t) & ((column >> 4) == h * 4 + l) & same16)
-                unperm[t, :, (h * 3 + l) * 128:(h * 3 + l + 1) * 128] = one_hot(
-                    ((column >> 4) == t) & ((row >> 4) == h * 4 + l) & same16)
 
     for load in loads:
         load.wait()
@@ -143,9 +135,9 @@
         return (owner & 7) * 16 + (owner >> 3) * 4 + slot
 
     row = lax.broadcasted_iota(I32, (16, 128), 0)
-    codes = jnp.where(row == 0, place(index_in[0], index_in[1]), 0)
-    codes = jnp.where(row == 1, place(graph, index_in[2]), codes)
-    codes = jnp.where(row == 2, index_in[3], codes).astype(F32).astype(BF16)
+    codes = jnp.where(row == x * 4, place(index_in[0], index_in[1]), 0)
+    codes = jnp.where(row == x * 4 + 1, place(graph, index_in[2]), codes)
+    codes = jnp.where(row == x * 4 + 2, index_in[3], codes).astype(F32).astype(BF16)
     for xb in range(NX):
         at = slice(xb * 128, (xb + 1) * 128)
         atx_out = at48[0, :, at].astype(BF16)
@@ -212,27 +204,33 @@
         a_ref[z, :, :, xb * 128:(xb + 1) * 128] = dot(order[...], stacked).astype(BF16).reshape(9, 16, 128)
 
     def right_copy(s):
-        slot = lax.rem(z - s + NZ, NZ)
-        return remote(PH_ATR, s, a_ref.at[slot], a_ref.at[slot], device(dz=1))
+        block = a_ref.at[lax.rem(z - s + NZ, NZ)]
+        block = block.at[pl.ds(0, 5)] if s == 3 else block
+        return remote(PH_ATR, s, block, block, device(dz=1))
 
     def left_copy(s):
-        slot = lax.rem(z + s, NZ)
-        return remote(PH_ATL, s, a_ref.at[slot], a_ref.at[slot], device(dz=NZ - 1))
+        block = a_ref.at[lax.rem(z + s, NZ)]
+        block = block.at[pl.ds(5, 4)] if s == 3 else block
+        return remote(PH_ATL, s, block, block, device(dz=NZ - 1))
+
+    right_copy(0).start()
+    left_copy(0).start()
 
     arrived(PH_COX, 0, cox.at[pl.ds(0, NX - 1)])
     stacked = jnp.concatenate([cox[s, 0:48] for s in range(NX)], axis=0)
+    codes = cox[0, 48:64].astype(F32)
+    for s in range(1, NX):
+        codes = codes + cox[s, 48:64].astype(F32)
+    codes = codes.astype(BF16)
     for t in range(NZ):
         wide = (dot(stacked, spread[t]) * same[...]).astype(BF16)
         packed = dot(gather16[...], wide).astype(BF16)
         cobuf[t, 0] = packed[:, 0:128]
         cobuf[t, 1] = packed[:, 128:256]
-        for s in range(NX):
-            cobuf[t, 2 + s] = cox[s, 48:64]
+        cobuf[t, 2] = codes
     each(NZ, lambda d: remote(
         PH_COZ, 0, cobuf.at[lax.rem(z + d, NZ)], corecv.at[z], device(dz=d)).start())
     corecv[z] = cobuf[z]
-    right_copy(0).start()
-    left_copy(0).start()
 
     for h in range(2):
         arrived(PH_Y, 3 * h, yrecv.at[0, halves[h]])
@@ -276,10 +274,10 @@
         folded = (lax.broadcasted_iota(I32, (128, 128), 0) & 63).astype(F32)
         for q in range(NX):
             at = slice(q * 128, (q + 1) * 128)
-            codes = corecv[t, 2 + q].astype(F32)
-            oh[t, :, at] = one_hot(lanes == codes[0:1])
-            oh[NZ, :, at] = one_hot(lanes == codes[1:2])
-            oh[NZ + 1, :, at] = one_hot(folded == codes[2:3])
+            codes = corecv[t, 2].astype(F32)
+            oh[t, :, at] = one_hot(lanes == codes[q * 4:q * 4 + 1])
+            oh[NZ, :, at] = one_hot(lanes == codes[q * 4 + 1:q * 4 + 2])
+            oh[NZ + 1, :, at] = one_hot(folded == codes[q * 4 + 2:q * 4 + 3])
         ch[...] = dot(cs[...], oh[NZ])
         turns[t] = dot(rot2[...], oh[NZ + 1])
         for q in range(NX):
@@ -295,17 +293,15 @@
         right_copy(s - 1).wait_recv()
         right_copy(s).start()
         left_copy(s - 1).wait_recv()
-        if s < 3:
-            left_copy(s).start()
+        left_copy(s).start()
 
     pass_on(1)
     lax.fori_loop(0, 3, prepare, 0)
-    pass_on(2)
-    lax.fori_loop(3, 5, prepare, 0)
 
     for k, dy in enumerate(NEAR):
         arrived(PH_YX, k, yxrecv.at[k] if dy else yxrecv.at[k, pl.ds(0, NX - 1)])
-    packed = jnp.zeros((32, 1024), F32)
+    slot = lax.broadcasted_iota(I32, (32, 128), 1) >> 4
+    packed = [jnp.zeros((32, 128), F32) for t in range(NZ)]
     for l in range(3):
         for s in range(NX):
             total = yxrecv[0, s, l].astype(F32)
@@ -313,17 +309,22 @@
                 total = total + yxrecv[k, s, l].astype(F32)
             mx[s, l] = total.astype(BF16)
         for h in range(2):
-            packed = packed + dot(mx[2 * h:2 * h + 2, l].reshape(32, 128), perm[l, h])
-    packed = packed.astype(BF16)
-    for t in range(NZ):
-        mzbuf[t] = packed[:, t * 128:(t + 1) * 128].reshape(2, 16, 128)
+            block = mx[2 * h:2 * h + 2, l].reshape(32, 128).astype(F32)
+            for t in range(NZ):
+                shifted = roll16(block, h * 4 + l - t)
+                packed[t] = jnp.where(slot == h * 4 + l, shifted, packed[t])
+    for t in range(NZ):
+        mzbuf[t] = packed[t].astype(BF16).reshape(2, 16, 128)
     each(NZ, lambda d: remote(
         PH_MZ, 0, mzbuf.at[lax.rem(z + d, NZ)], wc.at[z], device(dz=d)).start())
     wc[z] = mzbuf[z]
     mc[z] = mx[...]
+    pass_on(2)
+    lax.fori_loop(3, 5, prepare, 0)
     pass_on(3)
     lax.fori_loop(5, 8, prepare, 0)
     right_copy(3).wait_recv()
+    left_copy(3).wait_recv()
     arrived(PH_MZ, 0, wc.at[pl.ds(0, NZ - 1)])
     each(NZ, lambda d: remote(PH_MC, 0, mx, mc.at[z], device(dz=d)).start())
 
@@ -389,14 +390,23 @@
         PH_GZ, 0, gbuf.at[lax.rem(z + d, NZ)], grecv.at[z], device(dz=d)).start())
     grecv[z] = gbuf[z]
 
+    row, column = grid_of(192, 16)
+    block, within = split48(row)
+    expand[...] = one_hot(column == block * 4 + (within & 3))
+    for t in range(NZ):
+        row, column = grid_of(256, 128)
+        fold[t] = one_hot(((column >> 4) == t) & ((row & 15) == (column & 15)))
+
     arrived(PH_SZ, 0, sgrecv.at[pl.ds(0, NZ - 1)])
-    rows = dot(sgrecv[0].reshape(32, 128), unperm[0])
-    for t in range(1, NZ):
-        rows = rows + dot(sgrecv[t].reshape(32, 128), unperm[t])
-    for s in range(NX):
-        for l in range(3):
-            at = (s // 2 * 3 + l) * 128
-            sg4[s, l] = rows[s % 2 * 16:s % 2 * 16 + 16, at:at + 128].astype(BF16)
+    blocks = [sgrecv[t].reshape(32, 128).astype(F32) for t in range(NZ)]
+    for l in range(3):
+        for h in range(2):
+            total = jnp.zeros((32, 128), F32)
+            for t in range(NZ):
+                total = jnp.where(slot == t, roll16(blocks[t], t - (h * 4 + l)), total)
+            total = total.astype(BF16)
+            sg4[2 * h, l] = total[0:16]
+            sg4[2 * h + 1, l] = total[16:32]
 
     for k in (0, 4, 1, 3, 2):
         dy = NEAR[k]
@@ -473,7 +483,6 @@
     end_copy.wait_send()
     for s in range(4):
         right_copy(s).wait_send()
-    for s in range(3):
         left_copy(s).wait_send()
     for phase, ref in ((PH_Y, ybuf), (PH_FW, forwarded)):
         for h in range(2):
@@ -535,13 +544,11 @@
             b16(NZ, 9, 16, 512),
             f32(1, 48, 512),
             b16(2 * NX, 64, 128),
-            b16(NZ, 6, 16, 128),
-            b16(NZ, 6, 16, 128),
+            b16(NZ, 3, 16, 128),
+            b16(NZ, 3, 16, 128),
             b16(192, 16),
             b16(NZ, 256, 128),
             b16(NZ, 128, 256),
-            b16(3, 2, 128, 1024),
-            b16(NZ, 128, 768),
             b16(144, 192),
             b16(16, 192),
             f32(192, 256),

time: 77.2 us -> 74.1 us (0.960)
  Pallas kernels: 73.2 us -> 70.1 us
    pallas_call x1, Pallas kernels: 73.2 us -> 70.1 us  [shards(): pl.pallas_call(kernel, out_shape=(jax.ShapeDtypeStruct((9, 4, 512), F32),...]
where the time goes in v4:
time: 74.1 us; the launch traced here: 73.9 us
  Pallas kernels  70.1 us (95%)
  local copies, waits for them, and re-layouts  3.14 us (4%)
    pallas_call x1, Pallas kernels, shards(): pl.pallas_call(kernel, out_shape=(jax.ShapeDtypeStruct((9, 4, 512), F32),...  70.1 us
    unnamed x2, local copies, waits for them, and re-layouts  3.14 us

profile of v4, /device:TPU:1, one launch (start us, length us, event | category | flops | bytes accessed | tf_op | source)
XLA Modules:
  0.0 73.9 jit_solution(7198099509860975160)
XLA Ops:
  0.6 70.1 %shard_map.104 = (f32[9,4,512]{2,1,0:T(4,128)}, f32[2,3,16,512]{3,2,1,0:T(8,128)}) custom-call(s32[16,32]{1,0:T(8,128)} %coef.1, bf16[2,3,16,512]{3,2,1,0:T(8,128)(2,1)} %w_hbm.1, bf16[9,4,512]{2,1,0:T(4,128)(2,1)} %bitcast.13, bf16[9,4,512]{2,1,0:T(4,128)(2,1)} %bitcast.14, s32[1,128]{1,0:T(1,128)} %bitcast.15, s32[1,128]{1,0:T(1,128)} %slot_hbm.1, ...), custom_call_target="tpu_custom_call" | custom-call | flops 2000000000 | bytes 1000000 | tf_op jit(solution)/shard_map/pallas_call | solution.py:518
  70.7 1.5 %copy.13 = f32[1,4,9,512]{3,1,2,0:T(4,128)} copy(f32[1,4,9,512]{3,1,2,0:T(4,128)} %bitcast.11) | data formatting | bytes 147456
  72.2 1.6 %copy.14 = f32[2,3,16,512]{3,2,1,0:T(8,128)} copy(f32[2,3,16,512]{3,2,1,0:T(8,128)} %get-tuple-element.9) | data formatting | bytes 393216

commit v5 on v4

--- a/solution.py
+++ b/solution.py
@@ -14,7 +14,7 @@
 NT = (((1,), (1,)), ((), ()))
 
 (PH_CORE, PH_Y, PH_YX, PH_ATX, PH_ATR, PH_ATL, PH_COX, PH_COZ, PH_MZ, PH_MC,
- PH_GZ, PH_GX, PH_SZ, PH_SYX, PH_FW, PH_END, PH_MCL) = range(17)
+ PH_GZ, PH_GX, PH_SZ, PH_SYX, PH_FW, PH_END, PH_ATR1, PH_ATL1, PH_AX) = range(19)
 NEAR = (-2, -1, 0, 1, 2)
 ENTRY = {}
 for _opening, _closing in SPANS:
@@ -54,7 +54,7 @@
     at48, atx, a_ref, co80, cox, cobuf, corecv,
     expand, fold, spread, order, gather16, same, rot2,
     hs, cs, hh, ch, grads_at, turns, oh, u_ref, g_acc, gbuf, grecv, gxbuf, gxrecv,
-    sgt, sgbuf, sgrecv, sg4, sgx, forwarded, endbuf, endrecv,
+    sgt, sgbuf, sgrecv, sg4, sgx, forwarded, near_sum, endbuf, endrecv,
     load_sem, send_sem, recv_sem,
 ):
     grp, graph = lax.axis_index("grp"), lax.axis_index("graph")
@@ -74,11 +74,8 @@
         )
 
     def each(count, body):
-        def step(d, carry):
+        for d in range(1, count):
             body(d)
-            return carry
-
-        lax.fori_loop(1, count, step, 0)
 
     def arrived(phase, slot, ref):
         pltpu.make_async_copy(ref, ref, recv_sem.at[phase, slot]).wait()
@@ -203,18 +200,24 @@
         stacked = jnp.concatenate([atx[s, xb] for s in range(NX)], axis=0)
         a_ref[z, :, :, xb * 128:(xb + 1) * 128] = dot(order[...], stacked).astype(BF16).reshape(9, 16, 128)
 
-    def right_copy(s):
-        block = a_ref.at[lax.rem(z - s + NZ, NZ)]
-        block = block.at[pl.ds(0, 5)] if s == 3 else block
-        return remote(PH_ATR, s, block, block, device(dz=1))
-
-    def left_copy(s):
-        block = a_ref.at[lax.rem(z + s, NZ)]
-        block = block.at[pl.ds(5, 4)] if s == 3 else block
-        return remote(PH_ATL, s, block, block, device(dz=NZ - 1))
-
-    right_copy(0).start()
-    left_copy(0).start()
+    def z_hop(way, s):
+        slot = lax.rem(z + (s if way else NZ - s), NZ)
+        common = pl.ds(0, 5) if s < 3 else (pl.ds(3, 2) if way else pl.ds(0, 3))
+        parts = [(PH_ATL if way else PH_ATR, common)]
+        if s < 3 or way:
+            parts.append((PH_ATL1 if way else PH_ATR1, pl.ds(5 + x, 1)))
+        return [
+            remote(phase, s, a_ref.at[slot, part], a_ref.at[slot, part], device(dz=NZ - 1 if way else 1))
+            for phase, part in parts
+        ]
+
+    def along_x(slot):
+        block = a_ref.at[slot, pl.ds(5 + x, 1)]
+        each(NX, lambda d: remote(PH_AX, 0, block, block, device(dx=d)).start())
+
+    for way in range(2):
+        for copy in z_hop(way, 0):
+            copy.start()
 
     arrived(PH_COX, 0, cox.at[pl.ds(0, NX - 1)])
     stacked = jnp.concatenate([cox[s, 0:48] for s in range(NX)], axis=0)
@@ -269,34 +272,36 @@
     def entries_of(t, at):
         return {key: turns[t, k:k + 1, at] for key, k in ENTRY.items()}
 
-    def prepare(t, carry):
+    def prepare(t):
         lanes = lax.broadcasted_iota(I32, (128, 128), 0).astype(F32)
         folded = (lax.broadcasted_iota(I32, (128, 128), 0) & 63).astype(F32)
         for q in range(NX):
             at = slice(q * 128, (q + 1) * 128)
             codes = corecv[t, 2].astype(F32)
             oh[t, :, at] = one_hot(lanes == codes[q * 4:q * 4 + 1])
-            oh[NZ, :, at] = one_hot(lanes == codes[q * 4 + 1:q * 4 + 2])
-            oh[NZ + 1, :, at] = one_hot(folded == codes[q * 4 + 2:q * 4 + 3])
-        ch[...] = dot(cs[...], oh[NZ])
-        turns[t] = dot(rot2[...], oh[NZ + 1])
+            oh[NZ + t % 2, :, at] = one_hot(lanes == codes[q * 4 + 1:q * 4 + 2])
+            oh[NZ + 2 + t % 2, :, at] = one_hot(folded == codes[q * 4 + 2:q * 4 + 3])
+        ch[t % 2] = dot(cs[...], oh[NZ + t % 2])
+        turns[t] = dot(rot2[...], oh[NZ + 2 + t % 2])
         for q in range(NX):
             at = slice(q * 128, (q + 1) * 128)
             entries = entries_of(t, at)
             for opening, closing in SPANS:
                 for i in range(opening, closing):
                     grads_at[t, i * 16:(i + 1) * 16, at] = turned(
-                        entries, lambda b: ch[b * 16:(b + 1) * 16, at], opening, closing, i)
-        return carry
+                        entries, lambda b: ch[t % 2, b * 16:(b + 1) * 16, at], opening, closing, i)
 
     def pass_on(s):
-        right_copy(s - 1).wait_recv()
-        right_copy(s).start()
-        left_copy(s - 1).wait_recv()
-        left_copy(s).start()
+        for way in range(2):
+            for copy in z_hop(way, s - 1):
+                copy.wait_recv()
+            for copy in z_hop(way, s):
+                copy.start()
+            along_x(lax.rem(z + (s if way else NZ - s), NZ))
 
     pass_on(1)
-    lax.fori_loop(0, 3, prepare, 0)
+    for t in range(0, 3):
+        prepare(t)
 
     for k, dy in enumerate(NEAR):
         arrived(PH_YX, k, yxrecv.at[k] if dy else yxrecv.at[k, pl.ds(0, NX - 1)])
@@ -320,11 +325,17 @@
     wc[z] = mzbuf[z]
     mc[z] = mx[...]
     pass_on(2)
-    lax.fori_loop(3, 5, prepare, 0)
+    for t in range(3, 5):
+        prepare(t)
     pass_on(3)
-    lax.fori_loop(5, 8, prepare, 0)
-    right_copy(3).wait_recv()
-    left_copy(3).wait_recv()
+    for t in range(5, 8):
+        prepare(t)
+    for way in (1, 0):
+        for copy in z_hop(way, 3):
+            copy.wait_recv()
+        if way:
+            along_x(lax.rem(z + 4, NZ))
+    arrived(PH_AX, 0, a_ref.at[pl.ds(0, NZ - 1), pl.ds(0, NX - 1)])
     arrived(PH_MZ, 0, wc.at[pl.ds(0, NZ - 1)])
     each(NZ, lambda d: remote(PH_MC, 0, mx, mc.at[z], device(dz=d)).start())
 
@@ -445,6 +456,13 @@
     gxrecv[0] = gxbuf[x]
     for k in (1, 2, 3):
         arrived(PH_SYX, k, sgx.at[k] if NEAR[k] else sgx.at[k, pl.ds(0, NX - 1)])
+    for e in range(4):
+        for s in range(NX):
+            total = None
+            for k, dy in enumerate(NEAR):
+                term = share(-dy, (other_first if e < 2 else own_first) + e % 2) * sgx[k, s].astype(F32)
+                total = term if total is None else total + term
+            near_sum[e, s] = total
     arrived(PH_GX, 0, gxrecv.at[pl.ds(0, NX - 1)])
     total = gxrecv[0].astype(F32)
     for s in range(1, NX):
@@ -457,23 +475,20 @@
     for slot in (1, 2):
         arrived(PH_FW, slot, forwarded.at[slot])
 
-    def expert_sum(expert, s):
-        total = None
-        for k, dy in enumerate(NEAR):
-            term = share(-dy, expert) * sgx[k, s].astype(F32)
-            total = term if total is None else total + term
+    def expert_sum(e, expert, s):
+        total = near_sum[e, s]
         for slot, dy in ((0, 4), (1, -3), (2, 3)):
             total = total + share(dy, expert) * forwarded[slot, s].astype(F32)
         return total
 
     for e in range(2):
         for s in range(NX):
-            endbuf[e, s] = expert_sum(other_first + e, s).astype(BF16)
+            endbuf[e, s] = expert_sum(e, other_first + e, s).astype(BF16)
     end_copy = remote(PH_END, 0, endbuf, endrecv, device(other=True))
     end_copy.start()
     for e in range(2):
         for s in range(NX):
-            ge_ref[e, :, :, s * 128:(s + 1) * 128] = expert_sum(own_first + e, s)
+            ge_ref[e, :, :, s * 128:(s + 1) * 128] = expert_sum(e + 2, own_first + e, s)
     end_copy.wait_recv()
     for e in range(2):
         for s in range(NX):
@@ -482,8 +497,10 @@
     core_copy.wait_send()
     end_copy.wait_send()
     for s in range(4):
-        right_copy(s).wait_send()
-        left_copy(s).wait_send()
+        for way in range(2):
+            for copy in z_hop(way, s):
+                copy.wait_send()
+    left(PH_AX, 0, a_ref.at[pl.ds(0, NZ - 1), pl.ds(0, NX - 1)])
     for phase, ref in ((PH_Y, ybuf), (PH_FW, forwarded)):
         for h in range(2):
             left(phase, 3 * h, ref.at[0, halves[h]])
@@ -556,10 +573,10 @@
             b16(144, 128),
             b16(144, 128),
             f32(NZ, 144, 512),
-            f32(144, 512),
+            f32(2, 144, 512),
             f32(NZ, 144, 512),
             f32(NZ, 40, 512),
-            b16(NZ + 2, 128, 512),
+            b16(NZ + 4, 128, 512),
             b16(NZ, 144, 512),
             f32(144, 128),
             b16(NZ, 16, 256),
@@ -572,11 +589,12 @@
             b16(NX, 3, 16, 128),
             b16(5, NX, 3, 16, 128),
             b16(3, NX, 3, 16, 128),
+            f32(4, NX, 3, 16, 128),
             b16(2, NX, 3, 16, 128),
             b16(2, NX, 3, 16, 128),
             pltpu.SemaphoreType.DMA((8,)),
-            pltpu.SemaphoreType.DMA((17, 5)),
-            pltpu.SemaphoreType.DMA((17, 5)),
+            pltpu.SemaphoreType.DMA((19, 5)),
+            pltpu.SemaphoreType.DMA((19, 5)),
         ],
         compiler_params=pltpu.CompilerParams(
             collective_id=0, has_side_effects=True, vmem_limit_bytes=60 * 1024 * 1024

time: 74.1 us -> 73.3 us (0.989)
  Pallas kernels: 70.1 us -> 69.3 us
    pallas_call x1, Pallas kernels: 70.1 us -> 69.3 us  [shards(): pl.pallas_call(kernel, out_shape=(jax.ShapeDtypeStruct((9, 4, 512), F32),...]
where the time goes in v5:
time: 73.3 us; the launch traced here: 73 us
  Pallas kernels  69.3 us (95%)
  local copies, waits for them, and re-layouts  3.14 us (4%)
    pallas_call x1, Pallas kernels, shards(): pl.pallas_call(kernel, out_shape=(jax.ShapeDtypeStruct((9, 4, 512), F32),...  69.3 us
    unnamed x2, local copies, waits for them, and re-layouts  3.14 us

profile of v5, /device:TPU:1, one launch (start us, length us, event | category | flops | bytes accessed | tf_op | source)
XLA Modules:
  0.0 73.0 jit_solution(17709404290855961449)
XLA Ops:
  0.6 69.3 %shard_map.104 = (f32[9,4,512]{2,1,0:T(4,128)}, f32[2,3,16,512]{3,2,1,0:T(8,128)}) custom-call(s32[16,32]{1,0:T(8,128)} %coef.1, bf16[2,3,16,512]{3,2,1,0:T(8,128)(2,1)} %w_hbm.1, bf16[9,4,512]{2,1,0:T(4,128)(2,1)} %bitcast.13, bf16[9,4,512]{2,1,0:T(4,128)(2,1)} %bitcast.14, s32[1,128]{1,0:T(1,128)} %bitcast.15, s32[1,128]{1,0:T(1,128)} %slot_hbm.1, ...), custom_call_target="tpu_custom_call" | custom-call | flops 2000000000 | bytes 1000000 | tf_op jit(solution)/shard_map/pallas_call | solution.py:535
  69.9 1.5 %copy.13 = f32[1,4,9,512]{3,1,2,0:T(4,128)} copy(f32[1,4,9,512]{3,1,2,0:T(4,128)} %bitcast.11) | data formatting | bytes 147456
  71.4 1.6 %copy.14 = f32[2,3,16,512]{3,2,1,0:T(8,128)} copy(f32[2,3,16,512]{3,2,1,0:T(8,128)} %get-tuple-element.9) | data formatting | bytes 393216

commit v6 on v5

--- a/solution.py
+++ b/solution.py
@@ -14,7 +14,7 @@
 NT = (((1,), (1,)), ((), ()))
 
 (PH_CORE, PH_Y, PH_YX, PH_ATX, PH_ATR, PH_ATL, PH_COX, PH_COZ, PH_MZ, PH_MC,
- PH_GZ, PH_GX, PH_SZ, PH_SYX, PH_FW, PH_END, PH_ATR1, PH_ATL1, PH_AX) = range(19)
+ PH_GZ, PH_GX, PH_SZ, PH_SYX, PH_FW, PH_END, PH_ATR1, PH_ATL1, PH_AX, PH_MCF) = range(20)
 NEAR = (-2, -1, 0, 1, 2)
 ENTRY = {}
 for _opening, _closing in SPANS:
@@ -105,21 +105,13 @@
         each(NX, lambda d: greet(device(dy=dy, dx=d)))
     each(NZ, lambda d: greet(device(dz=d)))
 
-    row, column = grid_of(144, 192)
-    block, within = split48(column)
-    order[...] = one_hot(
-        ((within >> 2) == (row >> 4)) & (((row >> 2) & 3) == block) & ((within & 3) == (row & 3)))
-    row, column = grid_of(16, 192)
-    block, within = split48(column)
-    gather16[...] = one_hot(row == block * 4 + (within & 3))
-    row, column = grid_of(192, 256)
-    block, within = split48(row)
-    same[...] = jnp.where((within >> 2) == (column >> 4), 1.0, 0.0)
-    for t in range(NZ):
-        row, column = grid_of(128, 256)
-        spread[t] = one_hot(((row >> 4) == t) & ((row & 15) == (column & 15)))
-
-    for load in loads:
+    loads[0].wait()
+    pl.semaphore_wait(barrier, 1 + 4 + 5 * (NX - 1) + (NZ - 1))
+
+    core_copy = remote(PH_CORE, 0, w_own, w_sib, device(other=True))
+    core_copy.start()
+
+    for load in loads[1:]:
         load.wait()
 
     for b in range(9):
@@ -143,15 +135,25 @@
         cox[NX + xb, 0:48, :] = cox_out
         cox[NX + xb, 48:64, :] = codes
 
-    pl.semaphore_wait(barrier, 1 + 4 + 5 * (NX - 1) + (NZ - 1))
-
-    core_copy = remote(PH_CORE, 0, w_own, w_sib, device(other=True))
-    core_copy.start()
     each(NX, lambda d: remote(PH_ATX, 0, atx.at[NX], atx.at[x], device(dx=d)).start())
     each(NX, lambda d: remote(
         PH_COX, 0, cox.at[NX + lax.rem(x + d, NX)], cox.at[x], device(dx=d)).start())
     atx[x] = atx[NX]
     cox[x] = cox[NX + x]
+
+    row, column = grid_of(144, 192)
+    block, within = split48(column)
+    order[...] = one_hot(
+        ((within >> 2) == (row >> 4)) & (((row >> 2) & 3) == block) & ((within & 3) == (row & 3)))
+    row, column = grid_of(16, 192)
+    block, within = split48(column)
+    gather16[...] = one_hot(row == block * 4 + (within & 3))
+    row, column = grid_of(192, 256)
+    block, within = split48(row)
+    same[...] = jnp.where((within >> 2) == (column >> 4), 1.0, 0.0)
+    for t in range(NZ):
+        row, column = grid_of(128, 256)
+        spread[t] = one_hot(((row >> 4) == t) & ((row & 15) == (column & 15)))
 
     core_copy.wait_recv()
 
@@ -305,7 +307,7 @@
 
     for k, dy in enumerate(NEAR):
         arrived(PH_YX, k, yxrecv.at[k] if dy else yxrecv.at[k, pl.ds(0, NX - 1)])
-    slot = lax.broadcasted_iota(I32, (32, 128), 1) >> 4
+    lane_slot = lax.broadcasted_iota(I32, (32, 128), 1) >> 4
     packed = [jnp.zeros((32, 128), F32) for t in range(NZ)]
     for l in range(3):
         for s in range(NX):
@@ -317,7 +319,7 @@
             block = mx[2 * h:2 * h + 2, l].reshape(32, 128).astype(F32)
             for t in range(NZ):
                 shifted = roll16(block, h * 4 + l - t)
-                packed[t] = jnp.where(slot == h * 4 + l, shifted, packed[t])
+                packed[t] = jnp.where(lane_slot == h * 4 + l, shifted, packed[t])
     for t in range(NZ):
         mzbuf[t] = packed[t].astype(BF16).reshape(2, 16, 128)
     each(NZ, lambda d: remote(
@@ -337,7 +339,9 @@
             along_x(lax.rem(z + 4, NZ))
     arrived(PH_AX, 0, a_ref.at[pl.ds(0, NZ - 1), pl.ds(0, NX - 1)])
     arrived(PH_MZ, 0, wc.at[pl.ds(0, NZ - 1)])
-    each(NZ, lambda d: remote(PH_MC, 0, mx, mc.at[z], device(dz=d)).start())
+    for k, dz in enumerate(NEAR):
+        if dz:
+            remote(PH_MC, k, mx, mc.at[z], device(dz=NZ + dz)).start()
 
     columns16 = jnp.concatenate(
         [jnp.concatenate([wc[t, s] for t in range(NZ)], axis=0) for s in range(2)], axis=0)
@@ -401,6 +405,14 @@
         PH_GZ, 0, gbuf.at[lax.rem(z + d, NZ)], grecv.at[z], device(dz=d)).start())
     grecv[z] = gbuf[z]
 
+    below, above = mc.at[lax.rem(z + NZ - 2, NZ)], mc.at[lax.rem(z + 2, NZ)]
+    arrived(PH_MC, 4, below)
+    arrived(PH_MC, 0, above)
+    for k, ref, dz in (
+        (0, below, 1), (1, above, NZ - 1), (2, below.at[halves[0]], 2), (3, above.at[halves[1]], NZ - 2),
+    ):
+        remote(PH_MCF, k, ref, ref, device(dz=dz)).start()
+
     row, column = grid_of(192, 16)
     block, within = split48(row)
     expand[...] = one_hot(column == block * 4 + (within & 3))
@@ -414,7 +426,7 @@
         for h in range(2):
             total = jnp.zeros((32, 128), F32)
             for t in range(NZ):
-                total = jnp.where(slot == t, roll16(blocks[t], t - (h * 4 + l)), total)
+                total = jnp.where(lane_slot == t, roll16(blocks[t], t - (h * 4 + l)), total)
             total = total.astype(BF16)
             sg4[2 * h, l] = total[0:16]
             sg4[2 * h + 1, l] = total[16:32]
@@ -441,7 +453,12 @@
     for slot, k, hop in ((1, 4, 1), (2, 0, -1)):
         remote(PH_FW, slot, sgx.at[k], forwarded.at[slot], device(dy=hop)).start()
 
-    arrived(PH_MC, 0, mc.at[pl.ds(0, NZ - 1)])
+    for k, dz in ((1, 1), (3, -1)):
+        arrived(PH_MC, k, mc.at[lax.rem(z + NZ + dz, NZ)])
+    arrived(PH_MCF, 0, mc.at[lax.rem(z + NZ - 3, NZ)])
+    arrived(PH_MCF, 1, mc.at[lax.rem(z + 3, NZ)])
+    for h in range(2):
+        arrived(PH_MCF, 2 + h, mc.at[lax.rem(z + 4, NZ), halves[h]])
     coefficient = split48(lax.broadcasted_iota(I32, (192, 128), 0))[1] >> 2
     parts = jnp.zeros((192, 512), F32)
     for l, (opening, closing) in enumerate(SPANS):
@@ -514,7 +531,10 @@
     left(PH_GX, 0, gxbuf.at[pl.ds(0, NX - 1)])
     left(PH_COZ, 0, cobuf.at[pl.ds(0, NZ - 1)])
     left(PH_MZ, 0, mzbuf.at[pl.ds(0, NZ - 1)])
-    left(PH_MC, 0, mc.at[pl.ds(0, NZ - 1)])
+    for k in (0, 1, 3, 4):
+        left(PH_MC, k, mx)
+    for slot, ref in enumerate((mx, mx, mx.at[halves[0]], mx.at[halves[1]])):
+        left(PH_MCF, slot, ref)
     left(PH_SZ, 0, sgbuf.at[pl.ds(0, NZ - 1)])
     left(PH_GZ, 0, gbuf.at[pl.ds(0, NZ - 1)])
 
@@ -593,8 +613,8 @@
             b16(2, NX, 3, 16, 128),
             b16(2, NX, 3, 16, 128),
             pltpu.SemaphoreType.DMA((8,)),
-            pltpu.SemaphoreType.DMA((19, 5)),
-            pltpu.SemaphoreType.DMA((19, 5)),
+            pltpu.SemaphoreType.DMA((20, 5)),
+            pltpu.SemaphoreType.DMA((20, 5)),
         ],
         compiler_params=pltpu.CompilerParams(
             collective_id=0, has_side_effects=True, vmem_limit_bytes=60 * 1024 * 1024

time: 73.3 us -> 71.5 us (0.975)
  Pallas kernels: 69.3 us -> 67.5 us
    pallas_call x1, Pallas kernels: 69.3 us -> 67.5 us  [shards(): pl.pallas_call(kernel, out_shape=(jax.ShapeDtypeStruct((9, 4, 512), F32),...]
where the time goes in v6:
time: 71.5 us; the launch traced here: 71.3 us
  Pallas kernels  67.5 us (94%)
  local copies, waits for them, and re-layouts  3.14 us (4%)
    pallas_call x1, Pallas kernels, shards(): pl.pallas_call(kernel, out_shape=(jax.ShapeDtypeStruct((9, 4, 512), F32),...  67.5 us
    unnamed x2, local copies, waits for them, and re-layouts  3.14 us

profile of v6, /device:TPU:1, one launch (start us, length us, event | category | flops | bytes accessed | tf_op | source)
XLA Modules:
  0.0 71.3 jit_solution(15663054201128816514)
XLA Ops:
  0.6 67.5 %shard_map.104 = (f32[9,4,512]{2,1,0:T(4,128)}, f32[2,3,16,512]{3,2,1,0:T(8,128)}) custom-call(s32[16,32]{1,0:T(8,128)} %coef.1, bf16[2,3,16,512]{3,2,1,0:T(8,128)(2,1)} %w_hbm.1, bf16[9,4,512]{2,1,0:T(4,128)(2,1)} %bitcast.13, bf16[9,4,512]{2,1,0:T(4,128)(2,1)} %bitcast.14, s32[1,128]{1,0:T(1,128)} %bitcast.15, s32[1,128]{1,0:T(1,128)} %slot_hbm.1, ...), custom_call_target="tpu_custom_call" | custom-call | flops 2000000000 | bytes 1000000 | tf_op jit(solution)/shard_map/pallas_call | solution.py:555
  68.1 1.5 %copy.13 = f32[1,4,9,512]{3,1,2,0:T(4,128)} copy(f32[1,4,9,512]{3,1,2,0:T(4,128)} %bitcast.11) | data formatting | bytes 147456
  69.7 1.6 %copy.14 = f32[2,3,16,512]{3,2,1,0:T(8,128)} copy(f32[2,3,16,512]{3,2,1,0:T(8,128)} %get-tuple-element.9) | data formatting | bytes 393216

commit v7 on v6

--- a/solution.py
+++ b/solution.py
@@ -440,18 +440,18 @@
         each(NX, lambda d: remote(
             PH_SYX, k, sg4.at[lax.rem(x + d, NX)], sgx.at[k, x], device(dy=dy, dx=d)).start())
 
-    arrived(PH_GZ, 0, grecv.at[pl.ds(0, NZ - 1)])
-    held = jnp.zeros((192, 128), F32)
-    for t in range(NZ):
-        wide = (dot(expand[...], grecv[t]) * same[...]).astype(BF16)
-        held = held + dot(wide, fold[t])
-
     arrived(PH_SYX, 0, sgx.at[0])
     arrived(PH_SYX, 4, sgx.at[4])
     for h, k, hop in ((0, 0, -2), (1, 4, 2)):
         remote(PH_FW, 3 * h, sgx.at[k, halves[h]], forwarded.at[0, halves[h]], device(dy=hop)).start()
     for slot, k, hop in ((1, 4, 1), (2, 0, -1)):
         remote(PH_FW, slot, sgx.at[k], forwarded.at[slot], device(dy=hop)).start()
+
+    arrived(PH_GZ, 0, grecv.at[pl.ds(0, NZ - 1)])
+    held = jnp.zeros((192, 128), F32)
+    for t in range(NZ):
+        wide = (dot(expand[...], grecv[t]) * same[...]).astype(BF16)
+        held = held + dot(wide, fold[t])
 
     for k, dz in ((1, 1), (3, -1)):
         arrived(PH_MC, k, mc.at[lax.rem(z + NZ + dz, NZ)])

time: 71.5 us -> 72.5 us (1.014)
  Pallas kernels: 67.5 us -> 68.4 us
    pallas_call x1, Pallas kernels: 67.5 us -> 68.4 us  [shards(): pl.pallas_call(kernel, out_shape=(jax.ShapeDtypeStruct((9, 4, 512), F32),...]
where the time goes in v7:
time: 72.5 us; the launch traced here: 72.2 us
  Pallas kernels  68.4 us (94%)
  local copies, waits for them, and re-layouts  3.14 us (4%)
    pallas_call x1, Pallas kernels, shards(): pl.pallas_call(kernel, out_shape=(jax.ShapeDtypeStruct((9, 4, 512), F32),...  68.4 us
    unnamed x2, local copies, waits for them, and re-layouts  3.14 us

profile of v7, /device:TPU:1, one launch (start us, length us, event | category | flops | bytes accessed | tf_op | source)
XLA Modules:
  0.0 72.2 jit_solution(17909995124867192680)
XLA Ops:
  0.6 68.4 %shard_map.104 = (f32[9,4,512]{2,1,0:T(4,128)}, f32[2,3,16,512]{3,2,1,0:T(8,128)}) custom-call(s32[16,32]{1,0:T(8,128)} %coef.1, bf16[2,3,16,512]{3,2,1,0:T(8,128)(2,1)} %w_hbm.1, bf16[9,4,512]{2,1,0:T(4,128)(2,1)} %bitcast.13, bf16[9,4,512]{2,1,0:T(4,128)(2,1)} %bitcast.14, s32[1,128]{1,0:T(1,128)} %bitcast.15, s32[1,128]{1,0:T(1,128)} %slot_hbm.1, ...), custom_call_target="tpu_custom_call" | custom-call | flops 2000000000 | bytes 1000000 | tf_op jit(solution)/shard_map/pallas_call | solution.py:555
  69.1 1.5 %copy.13 = f32[1,4,9,512]{3,1,2,0:T(4,128)} copy(f32[1,4,9,512]{3,1,2,0:T(4,128)} %bitcast.11) | data formatting | bytes 147456
  70.6 1.6 %copy.14 = f32[2,3,16,512]{3,2,1,0:T(8,128)} copy(f32[2,3,16,512]{3,2,1,0:T(8,128)} %get-tuple-element.9) | data formatting | bytes 393216
